TPU v7x, 128 devices: a whole 4x4x4 slice. The times are simulated.
128 devices in a mesh: dp: 32 (over z, y, core), fsdp: 4 (over x).
Axes of the slice: x: 4, y: 4, z: 4, core: 2. Of those that a mesh axis runs over, the one named last changes fastest.
Arguments:
- tokens: bfloat16 [16384, 2048], P(('dp', 'fsdp')), may hold values from -24 to 24
- cotangent: bfloat16 [16384, 2048], P(('dp', 'fsdp')), may hold values from -24 to 24
- block_seq: int32 [32, 4], P('dp'), may hold values from 0 to 1, as said below
- seq_lengths: int32 [32, 2], P('dp'), may hold values from 1 to 384, as said below
- qkv_weight: float32 [2048, 6144], P(('dp', 'fsdp')), may hold values from -0.125 to 0.125
- qkv_moment: float32 [2048, 6144], P(('dp', 'fsdp')), may hold values from -64 to 64
- qkv_second: float32 [2048, 6144], P(('dp', 'fsdp')), may hold values from 4.096 to 65.536
- dense_weight: float32 [2048, 2048], P(('dp', 'fsdp')), may hold values from -0.375 to 0.375
- dense_moment: float32 [2048, 2048], P(('dp', 'fsdp')), may hold values from -16 to 16
- dense_second: float32 [2048, 2048], P(('dp', 'fsdp')), may hold values from 0.32768 to 5.24288
- expand_weight: float32 [2048, 8192], P(('dp', 'fsdp')), may hold values from -0.125 to 0.125
- expand_moment: float32 [2048, 8192], P(('dp', 'fsdp')), may hold values from -24 to 24
- expand_second: float32 [2048, 8192], P(('dp', 'fsdp')), may hold values from 0.73728 to 11.79648
- shrink_weight: float32 [8192, 2048], P(('dp', 'fsdp')), may hold values from -0.0625 to 0.0625
- shrink_moment: float32 [8192, 2048], P(('dp', 'fsdp')), may hold values from -48 to 48
- shrink_second: float32 [8192, 2048], P(('dp', 'fsdp')), may hold values from 2.94912 to 47.5136
- vectors: float32 [22528], P(('dp', 'fsdp')), may hold values from -1 to 1.5
- vec_moment: float32 [22528], P(('dp', 'fsdp')), may hold values from -80 to 80
- vec_second: float32 [22528], P(('dp', 'fsdp')), may hold values from 8.192 to 131.072
Outputs:
- output: bfloat16 [16384, 2048], P(('dp', 'fsdp'))
- input_grad: bfloat16 [16384, 2048], P(('dp', 'fsdp'))
- qkv_grad: float32 [2048, 6144], P(('dp', 'fsdp'))
- qkv_state: float32 [2048, 6144], P(('dp', 'fsdp'))
- qkv_new: float32 [2048, 6144], P(('dp', 'fsdp'))
- dense_grad: float32 [2048, 2048], P(('dp', 'fsdp'))
- dense_state: float32 [2048, 2048], P(('dp', 'fsdp'))
- dense_new: float32 [2048, 2048], P(('dp', 'fsdp'))
- expand_grad: float32 [2048, 8192], P(('dp', 'fsdp'))
- expand_state: float32 [2048, 8192], P(('dp', 'fsdp'))
- expand_new: float32 [2048, 8192], P(('dp', 'fsdp'))
- shrink_grad: float32 [8192, 2048], P(('dp', 'fsdp'))
- shrink_state: float32 [8192, 2048], P(('dp', 'fsdp'))
- shrink_new: float32 [8192, 2048], P(('dp', 'fsdp'))
- vec_grad: float32 [22528], P(('dp', 'fsdp'))
- vec_state: float32 [22528], P(('dp', 'fsdp'))
- vec_new: float32 [22528], P(('dp', 'fsdp'))
Inputs may be any that keep to these rules, and one draw needn't show every extreme that they name: `block_seq`: row g names, for each block of group g in row order, the sequence it holds; every sequence 0 to 1 holds one or more blocks, whose order in the row is the order of its positions; the first and the last block of a row hold the same sequence. `seq_lengths`: A sequence with c blocks has more than 128 * (c - 1) and at most 128 * c tokens; the rest of its last block is padding. In every group one sequence has exactly 128 * (3) tokens.
All inputs are finite; a program needn't handle non-finite values.
Results may differ from a plain program's by a relative error of at most 0.017.
Values may be sent and summed in bfloat16 or wider, within the bound.
A program may use at most 640 MiB of HBM per device.

v0:
```python
import jax
import jax.numpy as jnp
from jax import lax
from jax.sharding import Mesh
from jax.sharding import PartitionSpec as P

HEAD = 64
ROT = 32
BLOCK = 128
STEP = 10
DP_FSDP = ("dp_0", "dp_1", "dp_2", "fsdp")
DP = ("dp_0", "dp_1", "dp_2")


NORM_EPS = 1e-05
MASKED = -1e30
BETA_ONE = 0.9
BETA_TWO = 0.999
ADAM_EPS = 1e-08
RATES = (0.02, 0.1, 0.02, 0.01, 0.4)
DECAYS = (0.1, 0.1, 0.1, 0.1, 0.0)


def sent_together(arrays, axis, dim, along):
    both = jnp.concatenate(arrays, axis=along)
    result, at, gathered = (lax.all_gather(both, axis, axis=dim, tiled=True), 0, [])
    for a in arrays:
        gathered.append(lax.slice_in_dim(result, at, at + a.shape[along], axis=along))
        at += a.shape[along]
    return tuple(gathered)


def own_block(parts, axes, order):
    shape = [lax.axis_size(a) for a in axes]
    parts = parts.reshape(*shape, *parts.shape[1:])
    parts = parts.transpose(*order, *range(len(axes), parts.ndim))
    parts = parts.reshape(-1, *parts.shape[len(axes) :])
    for k in order:
        parts = lax.psum_scatter(parts, axes[k], scatter_dimension=0, tiled=True)
    return parts[0]


def cut_along(value, dim, length):
    shape = value.shape
    parts = value.reshape(*shape[:dim], length, shape[dim] // length, *shape[dim + 1 :])
    return jnp.moveaxis(parts, dim, 0)


def sum_by_axis(value, axes, order, dim):
    length = lax.axis_size(axes)
    return own_block(cut_along(value, dim, length), axes, order)


def sum_at_owner(value, axis, dim):
    parts = cut_along(value, dim, lax.axis_size(axis))
    arrived = lax.all_to_all(parts, axis, split_axis=0, concat_axis=0, tiled=True)
    return arrived.astype(jnp.float32).sum(axis=0)


def layer_norm(values, norm_gain, norm_shift):
    center = values - jnp.mean(values, axis=-1, keepdims=True)
    spread = jnp.mean(center * center, axis=-1, keepdims=True)
    return center * lax.rsqrt(spread + NORM_EPS) * norm_gain + norm_shift


def gelu_tanh(values):
    return jax.nn.gelu(values, approximate=True)


def rotary_tables(position, rot_dims):
    half_index = jnp.arange(rot_dims // 2, dtype=jnp.float32)
    inverse = 10000.0 ** (-2.0 * half_index / rot_dims)
    turned = position.astype(jnp.float32)[:, None] * inverse[None, :]
    return (jnp.cos(turned), jnp.sin(turned))


def rotate(values, cosine, sine_part):
    half_dims = cosine.shape[-1]
    front_part = values[..., :half_dims]
    second = values[..., half_dims : 2 * half_dims]
    cos_rows = cosine[:, None, :]
    sin_rows = sine_part[:, None, :]
    return jnp.concatenate(
        [
            front_part * cos_rows - second * sin_rows,
            second * cos_rows + front_part * sin_rows,
            values[..., 2 * half_dims :],
        ],
        axis=-1,
    )


def token_meta(block_row, length_row):
    total_blocks = block_row.shape[0]
    seq_count = length_row.shape[0]
    matching = block_row[None, :] == block_row[:, None]
    earlier_mask = jnp.arange(total_blocks)[None, :] < jnp.arange(total_blocks)[:, None]
    ranking = jnp.sum(jnp.where(matching & earlier_mask, 1, 0), axis=1).astype(jnp.int32)
    offsets = jnp.arange(BLOCK, dtype=jnp.int32)
    position = (ranking[:, None] * BLOCK + offsets[None, :]).reshape(-1)
    sequence = jnp.broadcast_to(block_row[:, None], (total_blocks, BLOCK)).reshape(-1)
    chosen = sequence[:, None] == jnp.arange(seq_count, dtype=jnp.int32)[None, :]
    limits = jnp.sum(jnp.where(chosen, length_row[None, :], 0), axis=1)
    return (sequence, position, position < limits)


def split_vectors(vec_all, model_width, ff_width):
    norm_gain = vec_all[:model_width]
    norm_shift = vec_all[model_width : 2 * model_width]
    bias_qkv = vec_all[2 * model_width : 5 * model_width]
    bias_dense = vec_all[5 * model_width : 6 * model_width]
    bias_expand = vec_all[6 * model_width : 6 * model_width + ff_width]
    bias_shrink = vec_all[6 * model_width + ff_width :]
    return (norm_gain, norm_shift, bias_qkv, bias_dense, bias_expand, bias_shrink)


def unpack(gathered, model_width):
    qkv_full, dense_full, expand_full, shrink_view, vec_low = gathered
    return (
        qkv_full,
        dense_full,
        expand_full,
        shrink_view.reshape(-1, model_width),
        vec_low.astype(jnp.float32),
    )


def cross(left_rows, right_rows):
    return lax.dot_general(
        left_rows, right_rows, (((0,), (0,)), ((), ())), preferred_element_type=jnp.float32
    )


def masked_scores(queries, keys_all, allowed, score_scale):
    scores = (
        jnp.einsum("qhd,khd->hqk", queries, keys_all, preferred_element_type=jnp.float32)
        * score_scale
    )
    return jnp.where(allowed[None], scores, MASKED)


def attention_forward(queries, keys_all, values_all, allowed, score_scale):
    scores = masked_scores(queries, keys_all, allowed, score_scale)
    ceiling = jnp.max(scores, axis=-1, keepdims=True)
    weights = jnp.exp(scores - ceiling)
    totals = jnp.sum(weights, axis=-1, keepdims=True)
    probability = (weights / totals).astype(jnp.bfloat16)
    attended = jnp.einsum(
        "hqk,khd->qhd", probability, values_all, preferred_element_type=jnp.float32
    )
    return (attended, ceiling + jnp.log(totals))


def attention_backward(queries, keys_all, values_all, allowed, score_scale, log_total, d_attended):
    scores = masked_scores(queries, keys_all, allowed, score_scale)
    probability = jnp.exp(scores - log_total)
    d_prob = jnp.einsum("qhd,khd->hqk", d_attended, values_all, preferred_element_type=jnp.float32)
    inner_sum = jnp.sum(probability * d_prob, axis=-1, keepdims=True)
    d_scores = (probability * (d_prob - inner_sum)).astype(jnp.bfloat16)
    d_queries = (
        jnp.einsum("hqk,khd->qhd", d_scores, keys_all, preferred_element_type=jnp.float32)
        * score_scale
    )
    d_keys = (
        jnp.einsum("hqk,qhd->khd", d_scores, queries, preferred_element_type=jnp.float32)
        * score_scale
    )
    d_values = jnp.einsum(
        "hqk,qhd->khd",
        probability.astype(jnp.bfloat16),
        d_attended,
        preferred_element_type=jnp.float32,
    )
    return (d_queries, d_keys, d_values)


def adam_step(weight, moment, second, gradient, step_rate, step_decay):
    moment_new = BETA_ONE * moment + (1 - BETA_ONE) * gradient
    second_new = BETA_TWO * second + (1 - BETA_TWO) * gradient * gradient
    moment_hat = moment_new / (1 - BETA_ONE**STEP)
    second_hat = second_new / (1 - BETA_TWO**STEP)
    updated = weight - step_rate * (
        moment_hat / (jnp.sqrt(second_hat) + ADAM_EPS) + step_decay * weight
    )
    return (second_new, updated)


def shards(
    tokens,
    cotangent,
    block_seq,
    seq_lengths,
    qkv_weight,
    qkv_moment,
    qkv_second,
    dense_weight,
    dense_moment,
    dense_second,
    expand_weight,
    expand_moment,
    expand_second,
    shrink_weight,
    shrink_moment,
    shrink_second,
    vectors,
    vec_moment,
    vec_second,
):
    local_rows, model_width = tokens.shape
    ff_width = expand_weight.shape[1]
    head_count = model_width // HEAD
    shard_rows = qkv_weight.shape[0]
    ff_ratio = ff_width // model_width
    score_scale = HEAD ** (-0.5)
    qkv_low = qkv_weight.astype(jnp.bfloat16)
    dense_low = dense_weight.astype(jnp.bfloat16)
    expand_low = expand_weight.astype(jnp.bfloat16)
    shrink_low = shrink_weight.astype(jnp.bfloat16).reshape(shard_rows, -1)
    vec_low = vectors.astype(jnp.bfloat16)
    params = unpack(
        (
            *sent_together((qkv_low, dense_low, expand_low, shrink_low), DP_FSDP, 0, 1),
            lax.all_gather(vec_low, DP_FSDP, axis=0, tiled=True),
        ),
        model_width,
    )
    w_qkv, w_dense, w_expand, w_shrink, vec_all = params
    norm_gain, norm_shift, bias_qkv, bias_dense, bias_expand, bias_shrink = split_vectors(
        vec_all, model_width, ff_width
    )
    sequence, position, live = token_meta(block_seq[0], seq_lengths[0])
    row_start = lax.axis_index("fsdp") * local_rows
    my_seq = lax.dynamic_slice_in_dim(sequence, row_start, local_rows)
    my_pos = lax.dynamic_slice_in_dim(position, row_start, local_rows)
    my_live = lax.dynamic_slice_in_dim(live, row_start, local_rows)
    allowed = (
        (my_seq[:, None] == sequence[None, :])
        & (position[None, :] <= my_pos[:, None])
        & live[None, :]
    )
    cosine, sine_part = rotary_tables(my_pos, ROT)
    inputs = tokens.astype(jnp.float32)
    normed, norm_back = jax.vjp(layer_norm, inputs, norm_gain, norm_shift)
    normed_low = normed.astype(jnp.bfloat16)
    projected = jnp.dot(normed_low, w_qkv, preferred_element_type=jnp.float32) + bias_qkv
    queries = rotate(
        projected[:, :model_width].reshape(local_rows, head_count, HEAD), cosine, sine_part
    ).astype(jnp.bfloat16)
    keys_local = (
        rotate(
            projected[:, model_width : 2 * model_width].reshape(local_rows, head_count, HEAD),
            cosine,
            sine_part,
        )
        .astype(jnp.bfloat16)
        .reshape(local_rows, model_width)
    )
    values_local = projected[:, 2 * model_width :].astype(jnp.bfloat16)
    keys_group, values_group = (
        lax.all_gather(keys_local, "fsdp", axis=0, tiled=True),
        lax.all_gather(values_local, "fsdp", axis=0, tiled=True),
    )
    keys_all = keys_group.reshape(-1, head_count, HEAD)
    values_all = values_group.reshape(-1, head_count, HEAD)
    attended, log_total = attention_forward(queries, keys_all, values_all, allowed, score_scale)
    attended_low = attended.reshape(local_rows, model_width).astype(jnp.bfloat16)
    branch_attn = jnp.dot(attended_low, w_dense, preferred_element_type=jnp.float32) + bias_dense
    pre_act = jnp.dot(normed_low, w_expand, preferred_element_type=jnp.float32) + bias_expand
    act_value, act_back = jax.vjp(gelu_tanh, pre_act)
    act_low = act_value.astype(jnp.bfloat16)
    branch_mlp = jnp.dot(act_low, w_shrink, preferred_element_type=jnp.float32) + bias_shrink
    output = (inputs + branch_attn + branch_mlp).astype(jnp.bfloat16)
    d_out = cotangent * my_live.astype(jnp.bfloat16)[:, None]
    params = unpack(
        (
            *sent_together((qkv_low, dense_low, expand_low, shrink_low), DP_FSDP, 0, 1),
            lax.all_gather(vec_low, DP_FSDP, axis=0, tiled=True),
        ),
        model_width,
    )
    w_qkv, w_dense, w_expand, w_shrink, vec_all = params
    d_attended = (
        jnp.dot(d_out, w_dense.T, preferred_element_type=jnp.float32)
        .astype(jnp.bfloat16)
        .reshape(local_rows, head_count, HEAD)
    )
    d_act = jnp.dot(d_out, w_shrink.T, preferred_element_type=jnp.float32)
    d_pre = act_back(d_act)[0].astype(jnp.bfloat16)
    d_queries, d_keys_part, d_values_part = attention_backward(
        queries, keys_all, values_all, allowed, score_scale, log_total, d_attended
    )
    d_keys, d_values = (
        lax.psum_scatter(
            d_keys_part.reshape(-1, model_width).astype(jnp.bfloat16),
            "fsdp",
            scatter_dimension=0,
            tiled=True,
        ).astype(jnp.float32),
        lax.psum_scatter(
            d_values_part.reshape(-1, model_width).astype(jnp.bfloat16),
            "fsdp",
            scatter_dimension=0,
            tiled=True,
        ).astype(jnp.float32),
    )
    d_query_pre = rotate(d_queries, cosine, -sine_part).reshape(local_rows, model_width)
    d_key_pre = rotate(d_keys.reshape(local_rows, head_count, HEAD), cosine, -sine_part).reshape(
        local_rows, model_width
    )
    d_qkv = jnp.concatenate([d_query_pre, d_key_pre, d_values], axis=1).astype(jnp.bfloat16)
    d_normed = jnp.dot(d_qkv, w_qkv.T, preferred_element_type=jnp.float32) + jnp.dot(
        d_pre, w_expand.T, preferred_element_type=jnp.float32
    )
    d_inputs, d_gain, d_shift = norm_back(d_normed)
    d_out_sum = jnp.sum(d_out, axis=0, dtype=jnp.float32)
    input_grad = (d_out.astype(jnp.float32) + d_inputs).astype(jnp.bfloat16)
    vec_terms = jnp.concatenate(
        [
            d_gain,
            d_shift,
            jnp.sum(d_qkv, axis=0, dtype=jnp.float32),
            d_out_sum,
            jnp.sum(d_pre, axis=0, dtype=jnp.float32),
            d_out_sum,
        ]
    )
    vec_grad = sum_by_axis(vec_terms, DP_FSDP, (2, 0, 1, 3), 0)
    qkv_term = cross(normed_low, d_qkv)
    dense_term = cross(attended_low, d_out)
    expand_term = cross(normed_low, d_pre)
    shrink_term = cross(act_low, d_out).reshape(
        shard_rows * lax.axis_size("fsdp") * lax.axis_size(DP), ff_ratio * model_width
    )
    group_sums = lax.psum_scatter(
        jnp.concatenate([qkv_term, dense_term, expand_term, shrink_term], axis=1).astype(
            jnp.bfloat16
        ),
        DP,
        scatter_dimension=0,
        tiled=True,
    )
    all_grads = sum_at_owner(group_sums, "fsdp", 0)
    qkv_grad = all_grads[:, : 3 * model_width]
    dense_grad = all_grads[:, 3 * model_width : 4 * model_width]
    expand_grad = all_grads[:, 4 * model_width : 4 * model_width + ff_width]
    shrink_grad = all_grads[:, 4 * model_width + ff_width :].reshape(-1, model_width)
    masters = (qkv_weight, dense_weight, expand_weight, shrink_weight, vectors)
    moments = (qkv_moment, dense_moment, expand_moment, shrink_moment, vec_moment)
    seconds = (qkv_second, dense_second, expand_second, shrink_second, vec_second)
    gradients = (qkv_grad, dense_grad, expand_grad, shrink_grad, vec_grad)
    results = [output, input_grad]
    for index_w in range(5):
        state_new, weight_new = adam_step(
            masters[index_w],
            moments[index_w],
            seconds[index_w],
            gradients[index_w],
            RATES[index_w],
            DECAYS[index_w],
        )
        results.extend([gradients[index_w], state_new, weight_new])
    return tuple(results)


def solution(mesh):
    finer = Mesh(
        mesh.devices.reshape(4, 4, 2, mesh.shape["fsdp"]), ("dp_0", "dp_1", "dp_2", "fsdp")
    )
    return jax.shard_map(
        shards,
        mesh=finer,
        in_specs=(
            P(DP_FSDP, None),
            P(DP_FSDP, None),
            P(DP, None),
            P(DP, None),
            P(DP_FSDP, None),
            P(DP_FSDP, None),
            P(DP_FSDP, None),
            P(DP_FSDP, None),
            P(DP_FSDP, None),
            P(DP_FSDP, None),
            P(DP_FSDP, None),
            P(DP_FSDP, None),
            P(DP_FSDP, None),
            P(DP_FSDP, None),
            P(DP_FSDP, None),
            P(DP_FSDP, None),
            P(DP_FSDP),
            P(DP_FSDP),
            P(DP_FSDP),
        ),
        out_specs=(
            P(DP_FSDP, None),
            P(DP_FSDP, None),
            P(DP_FSDP, None),
            P(DP_FSDP, None),
            P(DP_FSDP, None),
            P(DP_FSDP, None),
            P(DP_FSDP, None),
            P(DP_FSDP, None),
            P(DP_FSDP, None),
            P(DP_FSDP, None),
            P(DP_FSDP, None),
            P(DP_FSDP, None),
            P(DP_FSDP, None),
            P(DP_FSDP, None),
            P(DP_FSDP),
            P(DP_FSDP),
            P(DP_FSDP),
        ),
        check_vma=False,
    )
```

profile of v0, /device:TPU:1, one launch (start us, length us, event | category | flops | bytes accessed | tf_op | source)
XLA Modules:
  0.0 1138.4 jit_solution(6110350574343681882)
XLA Ops:
  12.9 70.6 %all-reduce = bf16[22528]{0:T(1024)(128)(2,1)S(1)} all-reduce(bf16[22528]{0:T(1024)(128)(2,1)S(1)} %dynamic-update-slice), channel_id=1, replica_groups=mesh['dp_0'=4,'dp_1'=4,'dp_2'=2,'fsdp'=4] {'dp_0','dp_1','dp_2','fsdp'}, use_global_device_ids=true, to_apply=%add | all-reduce | flops 22528 | bytes 90112
  85.7 155.4 %all-gather.4.cloned.1.call-done = bf16[2048,24576]{1,0:T(8,128)(2,1)} async-done(((bf16[16,24576]{1,0:T(8,128)(2,1)}), bf16[2048,24576]{1,0:T(8,128)(2,1)}) %all-gather.4.cloned.1.call-update) | async-done | bytes 100663312 | tf_op jit(solution)/shard_map/all_gather | solution.py:26
  241.0 10.1 fusion.16
  260.7 6.3 fusion.44
  268.6 15.3 %fusion.8 = f32[128,8192]{1,0:T(8,128)} fusion(bf16[2048,24576]{1,0:T(8,128)(2,1)} %all-gather.4.cloned.1.call-done, f32[8192]{0:T(1024)S(1)} %slice.141, bf16[128,2048]{1,0:T(8,128)(2,1)S(1)} %copy-done.3, f32[2048]{0:T(1024)S(1)} %get-tuple-element.51, f32[2048]{0:T(1024)S(1)} %get-tuple-element.50, f32[128]{0:T(128)S(1)} %fusion.76, ...), kind=kOutput, calls=%fused_computation.12 | convolution fusion | flops 4297588736 | bytes 38323200 | tf_op jit(solution)/shard_map/dot_general | solution.py:268
  296.7 28.4 %all-gather.6.cloned.1.call-done = bf16[512,2048]{1,0:T(8,128)(2,1)} async-done(((bf16[128,2048]{1,0:T(8,128)(2,1)}), bf16[512,2048]{1,0:T(8,128)(2,1)}) %all-gather.6.cloned.1.call-update) | async-done | bytes 2097168 | tf_op jit(solution)/shard_map/all_gather | solution.py:261
  328.0 6.8 multiply_reduce_fusion
  345.5 16.3 %convolution_convert_fusion.1 = bf16[8192,2048]{1,0:T(8,128)(2,1)} fusion(bf16[128,2048]{1,0:T(8,128)(2,1)S(1)} %copy-done.4, bf16[128]{0:T(256)(128)(2,1)S(1)} %dynamic-slice_convert_fusion, f32[128,8192]{1,0:T(8,128)} %fusion.8), kind=kOutput, calls=%fused_computation.2 | convolution fusion | flops 4321443840 | bytes 38273280 | tf_op jit(solution)/shard_map/dot_general | solution.py:129
  361.8 23.1 %slice.142 = bf16[2048,8192]{1,0:T(8,128)(2,1)} slice(bf16[2048,24576]{1,0:T(8,128)(2,1)} %all-gather.4.cloned.1.call-done), slice={[0:2048], [16384:24576]} | slice | bytes 67108864 | tf_op jit(solution)/shard_map/slice | solution.py:28
  384.9 55.1 %reshape.324 = bf16[8192,2048]{1,0:T(8,128)(2,1)} reshape(bf16[2048,8192]{1,0:T(8,128)(2,1)} %slice.142) | data formatting | bytes 67108864 | tf_op jit(solution)/shard_map/reshape | solution.py:123
  440.0 55.0 %reshape.330 = bf16[2048,8192]{1,0:T(8,128)(2,1)} reshape(bf16[8192,2048]{1,0:T(8,128)(2,1)} %convolution_convert_fusion.1) | data formatting | bytes 67108864 | tf_op jit(solution)/shard_map/reshape | solution.py:331
  495.0 19.6 %convert_reduce_fusion.1 = (f32[8192]{0:T(1024)}, bf16[128,8192]{1,0:T(8,128)(2,1)}) fusion(f32[128,8192]{1,0:T(8,128)} %fusion.8, bf16[8192,2048]{1,0:T(8,128)(2,1)} %reshape.324, bf16[128,2048]{1,0:T(8,128)(2,1)S(1)} %copy-done.4, bf16[128]{0:T(256)(128)(2,1)S(1)} %dynamic-slice_convert_fusion), kind=kOutput, calls=%fused_computation.38 | convolution fusion | flops 4318289920 | bytes 40403200 | tf_op jit(solution)/shard_map/dot_general | solution.py:287
  514.6 7.2 fusion.50
  526.1 15.9 %convolution_convert_fusion = bf16[2048,8192]{1,0:T(8,128)(2,1)} fusion(bf16[128,8192]{1,0:T(8,128)(2,1)} %get-tuple-element.66, bf16[128,2048]{1,0:T(8,128)(2,1)S(1)} %copy-done.3, f32[2048]{0:T(1024)S(1)} %get-tuple-element.51, f32[2048]{0:T(1024)S(1)} %get-tuple-element.50, f32[128]{0:T(128)S(1)} %fusion.76, f32[128]{0:T(128)S(1)} %broadcast_multiply_fusion.2), kind=kOutput, calls=%fused_computation.1 | convolution fusion | flops 4313317376 | bytes 36193280 | tf_op jit(solution)/shard_map/dot_general | solution.py:129
  557.7 12.4 %copy.70 = bf16[2048,2048]{1,0:T(8,128)(2,1)} copy(bf16[2048,2048]{0,1:T(8,128)(2,1)} %convolution_convert_fusion.3) | data formatting | bytes 16777216 | tf_op jit(solution)/shard_map/convert.2
  573.2 14.6 %convolution_convert_fusion.2 = bf16[2048,6144]{1,0:T(8,128)(2,1)} fusion(bf16[128,2048]{0,1:T(8,128)(2,1)S(1)} %copy.75, bf16[128,2048]{0,1:T(8,128)(2,1)S(1)} %bitcast.59, bf16[128,2048]{0,1:T(8,128)(2,1)S(1)} %bitcast.56, bf16[128,2048]{1,0:T(8,128)(2,1)S(1)} %copy-done.3, f32[2048]{0:T(1024)S(1)} %get-tuple-element.51, f32[2048]{0:T(1024)S(1)} %get-tuple-element.50, ...), kind=kOutput, calls=%fused_computation.7 | convolution fusion | flops 3240099840 | bytes 27280384 | tf_op jit(solution)/shard_map/dot_general | solution.py:129
  587.8 65.7 %pad_maximum_fusion = bf16[2048,24576]{1,0:T(8,128)(2,1)} fusion(bf16[2048,8192]{1,0:T(8,128)(2,1)} %reshape.330, bf16[2048,8192]{1,0:T(8,128)(2,1)} %convolution_convert_fusion, bf16[2048,2048]{1,0:T(8,128)(2,1)} %copy.70, bf16[2048,6144]{1,0:T(8,128)(2,1)} %convolution_convert_fusion.2), kind=kLoop, calls=%fused_computation | loop fusion | flops 402653184 | bytes 201326592 | tf_op jit(solution)/shard_map/concatenate | solution.py:335
  656.0 21.2 %fusion = f32[128,2048]{1,0:T(8,128)} fusion(bf16[128,8192]{1,0:T(8,128)(2,1)} %get-tuple-element.66, bf16[2048,24576]{1,0:T(8,128)(2,1)} %all-gather.4.cloned.1.call-done), kind=kOutput, calls=%fused_computation.3 | convolution fusion | flops 4294967296 | bytes 36700160 | tf_op jit(solution)/shard_map/dot_general | solution.py:311
  677.2 23.0 %fusion.90 = (f32[2048]{0:T(1024)S(1)}, f32[128]{0:T(128)S(1)}, f32[128,2048]{1,0:T(8,128)}) fusion(f32[2048]{0:T(1024)S(1)} %get-tuple-element.50, f32[128]{0:T(128)S(1)} %broadcast_multiply_fusion.2, bf16[128,2048]{1,0:T(8,128)(2,1)S(1)} %copy-done.3, f32[128,2048]{1,0:T(8,128)} %fusion, bf16[2048,24576]{1,0:T(8,128)(2,1)} %all-gather.4.cloned.1.call-done, ...), kind=kOutput, calls=%fused_computation.145 | convolution fusion | flops 3227777024 | bytes 29377536 | tf_op jit(solution)/shard_map/dot_general | solution.py:311
  706.7 349.7 %reduce-scatter.10.cloned.1.call-done = bf16[64,24576]{1,0:T(8,128)(2,1)} async-done(((bf16[2048,24576]{1,0:T(8,128)(2,1)}), bf16[64,24576]{1,0:T(8,128)(2,1)}) %reduce-scatter.10.cloned.1.call-update) | async-done | bytes 3145744 | tf_op jit(solution)/shard_map/reduce_scatter | solution.py:334
  1061.1 15.0 %convolution_add_fusion = f32[128,2048]{1,0:T(8,128)S(1)} fusion(bf16[8192,2048]{1,0:T(8,128)(2,1)} %reshape.324, f32[2048]{0:T(1024)S(1)} %copy-done.23, f32[128,8192]{1,0:T(8,128)} %fusion.8), kind=kOutput, calls=%fused_computation.49 | convolution fusion | flops 4304666624 | bytes 38805504 | tf_op jit(solution)/shard_map/dot_general | solution.py:271
  1081.7 13.8 %reduce-scatter.14.cloned.1.call-done = f32[16,176]{1,0:T(8,128)} async-done(((f32[64,176]{1,0:T(8,128)}), f32[16,176]{1,0:T(8,128)}) %reduce-scatter.14.cloned.1.call-update) | async-done | bytes 11280 | tf_op jit(solution)/shard_map/reduce_scatter | solution.py:39
  1095.5 14.1 %all-reduce.1 = f32[16,176]{1,0:T(8,128)S(1)} all-reduce(f32[16,176]{1,0:T(8,128)} %reduce-scatter.14.cloned.1.call-done), channel_id=7, replica_groups=mesh['dp_0'=4,'dp_1'=4,'dp_2'=2,'fsdp'=4] {'dp_1'}, use_global_device_ids=true, to_apply=%region_20.21.clone | all-reduce | flops 2816 | bytes 22528
  1109.6 8.5 all-reduce.2
  (178 shorter events, 99.6 us)
Async XLA Ops:
  7.2 76.3 %copy-start.29 = (s32[1,4]{1,0:T(1,128)S(1)}, s32[1,4]{1,0:T(1,128)}, u32[]{:S(2)}) copy-start(s32[1,4]{1,0:T(1,128)} %param.21) | copy-start | bytes 52
  7.2 76.6 %copy-start.3 = (bf16[128,2048]{1,0:T(8,128)(2,1)S(1)}, bf16[128,2048]{1,0:T(8,128)(2,1)}, u32[]{:S(2)}) copy-start(bf16[128,2048]{1,0:T(8,128)(2,1)} %param.19) | copy-start | bytes 1572868
  7.2 233.8 %all-gather.4.cloned.1.call-start = ((), (), s32[]{:S(2)}) async-start(), calls=%async_computation.6 | async-start | bytes 101449728 | tf_op jit(solution)/shard_map/all_gather | solution.py:26
  12.6 277.6 %all-gather.8.cloned.1.call-start = ((), (), s32[]{:S(2)}) async-start(), calls=%async_computation.8 | async-start | bytes 2621440 | tf_op jit(solution)/shard_map/all_gather | solution.py:260
  84.3 166.9 %copy-start.31 = (f32[128]{0:T(128)}, f32[128]{0:T(128)S(1)}, u32[]{:S(2)}) copy-start(f32[128]{0:T(128)S(1)} %fusion.65) | copy-start | bytes 1540
  85.1 170.8 %copy-start.18 = (f32[128,16]{0,1:T(8,128)}, f32[128,16]{0,1:T(8,128)S(1)}, u32[]{:S(2)}) copy-start(f32[128,16]{0,1:T(8,128)S(1)} %get-tuple-element.59) | copy-start | bytes 24580
  257.0 33.1 %copy-start.12 = (bf16[128,32,16]{0,2,1:T(8,128)(2,1)}, bf16[128,32,16]{0,2,1:T(8,128)(2,1)S(1)}, u32[]{:S(2)}) copy-start(bf16[128,32,16]{0,2,1:T(8,128)(2,1)S(1)} %get-tuple-element.43) | copy-start | bytes 393220
  257.0 33.1 %copy-start.14 = (bf16[128,32,16]{0,2,1:T(8,128)(2,1)}, bf16[128,32,16]{0,2,1:T(8,128)(2,1)S(1)}, u32[]{:S(2)}) copy-start(bf16[128,32,16]{0,2,1:T(8,128)(2,1)S(1)} %get-tuple-element.44) | copy-start | bytes 393220
  257.9 67.2 %all-gather.6.cloned.1.call-start = ((), (), s32[]{:S(2)}) async-start(), calls=%async_computation.7 | async-start | bytes 2621440 | tf_op jit(solution)/shard_map/all_gather | solution.py:261
  268.0 302.1 %reduce-scatter.16.cloned.1.call-start = ((), (), s32[]{:S(2)}) async-start(), calls=%async_computation.12 | async-start | bytes 2621440
  345.3 226.6 %reduce-scatter.18.cloned.1.call-start = ((), (), s32[]{:S(2)}) async-start(), calls=%async_computation.13 | async-start | bytes 2621440
  525.8 530.6 %reduce-scatter.10.cloned.1.call-start = ((), (), s32[]{:S(2)}) async-start(), calls=%async_computation.9 | async-start | bytes 103809024 | tf_op jit(solution)/shard_map/reduce_scatter | solution.py:334
  526.1 15.9 %copy-start.2 = (bf16[32,128,512]{2,1,0:T(8,128)(2,1)S(1)}, bf16[32,128,512]{2,1,0:T(8,128)(2,1)}, u32[]{:S(2)}) copy-start(bf16[32,128,512]{2,1,0:T(8,128)(2,1)} %copy-done.1) | copy-start | bytes 12582916
  653.6 422.5 %reduce-scatter.12.cloned.1.call-start = ((), (), s32[]{:S(2)}) async-start(), calls=%async_computation.10 | async-start | bytes 196608 | tf_op jit(solution)/shard_map/reduce_scatter | solution.py:39
  677.2 23.0 %copy-start.32 = (f32[128]{0:T(128)S(1)}, f32[128]{0:T(128)}, u32[]{:S(2)}) copy-start(f32[128]{0:T(128)} %copy-done.31) | copy-start | bytes 1540
  705.7 355.4 %copy-start.23 = (f32[2048]{0:T(1024)S(1)}, f32[2048]{0:T(1024)}, u32[]{:S(2)}) copy-start(f32[2048]{0:T(1024)} %get-tuple-element.52) | copy-start | bytes 24580
  1056.4 63.0 %all-to-all-start = ((bf16[4,16,24576]{2,1,0:T(8,128)(2,1)}), bf16[4,16,24576]{2,1,0:T(8,128)(2,1)}, u32[]{:S(2)}, u32[]{:S(2)}) async-start(bf16[4,16,24576]{2,1,0:T(8,128)(2,1)} %bitcast.68), calls=%async_computation.1 | async-start | bytes 6291456 | tf_op jit(solution)/shard_map/all_to_all | solution.py:56
  1061.0 34.5 %reduce-scatter.14.cloned.1.call-start = ((), (), s32[]{:S(2)}) async-start(), calls=%async_computation.11 | async-start | bytes 81920 | tf_op jit(solution)/shard_map/reduce_scatter | solution.py:39
  1061.1 15.1 %copy-start.17 = (bf16[32,64,128]{2,1,0:T(8,128)(2,1)S(1)}, bf16[32,64,128]{2,1,0:T(8,128)(2,1)}, u32[]{:S(2)}) copy-start(bf16[32,64,128]{2,1,0:T(8,128)(2,1)} %copy-done.16) | copy-start | bytes 1572868
  1061.1 15.1 %copy-start.22 = (f32[2048]{0:T(1024)S(1)}, f32[2048]{0:T(1024)}, u32[]{:S(2)}) copy-start(f32[2048]{0:T(1024)} %get-tuple-element.49) | copy-start | bytes 24580
  1076.2 42.6 %copy-start.26 = (f32[176]{0:T(256)S(1)}, f32[176]{0:T(256)}, u32[]{:S(2)}) copy-start(f32[176]{0:T(256)} %param.35) | copy-start | bytes 2116
  1076.2 42.6 %copy-start.27 = (f32[176]{0:T(256)S(1)}, f32[176]{0:T(256)}, u32[]{:S(2)}) copy-start(f32[176]{0:T(256)} %param.36) | copy-start | bytes 2116
  1076.2 42.6 %copy-start.28 = (f32[176]{0:T(256)S(1)}, f32[176]{0:T(256)}, u32[]{:S(2)}) copy-start(f32[176]{0:T(256)} %param.37) | copy-start | bytes 2116
  1081.7 40.2 %copy-start.8 = (f32[16,8192]{1,0:T(8,128)S(1)}, f32[16,8192]{1,0:T(8,128)}, u32[]{:S(2)}) copy-start(f32[16,8192]{1,0:T(8,128)} %param.29) | copy-start | bytes 1572868
  (22 other events, 121.6 us)
Sparse Core Ops, SparseCore 0:
  12.7 228.2 all-gather.3
  258.1 32.0 all-gather.7
  292.4 32.6 all-gather.5
  345.4 29.7 reduce-scatter.15
  525.9 29.9 reduce-scatter.17
  653.7 402.6 reduce-scatter.9
  1059.3 10.2 reduce-scatter.11
  1076.3 19.1 reduce-scatter.13
where the time goes:
time: 1150 us; the launch traced here: 1140 us
  waiting for transfers between devices  554 us (48%)
  matrix products  196 us (17%)
  local copies, waits for them, and re-layouts  176 us (15%)
  other arithmetic  97.5 us (8%)
  blocking collectives  93.1 us (8%)
  between operations  15.7 us (1%)
    reduce_scatter x1, waiting for transfers between devices, shards(): lax.psum_scatter(jnp.concatenate([qkv_term, dense_term, expand_term, shri...  350 us
    all_gather x1, waiting for transfers between devices, sent_together(): lax.all_gather(both, axis, axis=dim, tiled=True)  155 us
    unnamed x3, blocking collectives  93.1 us
    concatenate x1, other arithmetic, shards(): jnp.concatenate([qkv_term, dense_term, expand_term, shrink_term], axis=1)  65.7 us
    reshape x1, local copies, waits for them, and re-layouts, unpack(): shrink_view.reshape(-1, model_width)  55.1 us
    reshape x1, local copies, waits for them, and re-layouts, shards(): cross(act_low, d_out)  55 us
    dot_general x4, matrix products, cross(): lax.dot_general(left_rows, right_rows, (((0,), (0,)), ((), ())), preferre...  52.5 us
    all_gather x1, waiting for transfers between devices, shards(): lax.all_gather(values_local, 'fsdp', axis=0, tiled=True)  28.4 us
  transfers between devices with their start and end apart: 9, of which 5 were waited for; matrix products, arithmetic and copies ran while one was open for 29% of the time, Pallas kernels for 0%

commit v1 on v0

v1 whole, which is shorter than its diff:
```python
import functools

import jax
import jax.numpy as jnp
import numpy as np
from jax import lax
from jax.experimental import pallas as pl
from jax.experimental.pallas import tpu as pltpu
from jax.sharding import Mesh
from jax.sharding import PartitionSpec as P

HEAD = 64
ROT = 32
BLOCK = 128
STEP = 10
GROUP = 512
MODEL = 2048
FF = 8192
PAIR = 2 * HEAD
ALL = ("z", "y", "c", "x")
DP = ("z", "y", "c")
ZY = ("z", "y")
TP = ("c", "x")
SIZES = (4, 4, 2, 4)
TPN = 8
SCALE = HEAD ** (-0.5)

NORM_EPS = 1e-05
MASKED = -1e30
BETA_ONE = 0.9
BETA_TWO = 0.999
ADAM_EPS = 1e-08
RATES = (0.02, 0.1, 0.02, 0.01, 0.4)
DECAYS = (0.1, 0.1, 0.1, 0.1, 0.0)
GELU_A = float(np.sqrt(2.0 / np.pi))
GELU_B = 0.044715


def dot(a, b):
    return jnp.dot(a, b, preferred_element_type=jnp.float32)


def dot_t(a, b):
    return lax.dot_general(a, b, (((1,), (1,)), ((), ())), preferred_element_type=jnp.float32)


def cross(a, b):
    return lax.dot_general(a, b, (((0,), (0,)), ((), ())), preferred_element_type=jnp.float32)


def rotary_constants():
    half = np.arange(ROT // 2, dtype=np.float32)
    inverse = (10000.0 ** (-2.0 * half.astype(np.float64) / ROT)).astype(np.float32)
    angle = (np.arange(GROUP, dtype=np.float32)[:, None] * inverse[None, :]).astype(np.float64)
    cosine, sine = np.cos(angle).astype(np.float32), np.sin(angle).astype(np.float32)
    one = np.ones((GROUP, HEAD - ROT), np.float32)
    zero = np.zeros((GROUP, ROT // 2), np.float32)
    rest = np.zeros((GROUP, HEAD - ROT), np.float32)
    turn = np.concatenate([cosine, cosine, one], axis=1)
    ahead = np.concatenate([-sine, zero, rest], axis=1)
    behind = np.concatenate([zero, sine, rest], axis=1)
    return tuple(np.concatenate([a, a], axis=1) for a in (turn, ahead, behind))


def device_number(z, y, c, x):
    return ((z * 4 + y) * 2 + c) * 4 + x


def dense_route():
    pairs = []
    for z, y, c, x in np.ndindex(*SIZES):
        pairs.append((device_number(z, y, c, x), device_number((z // 2) * 2 + c, x, z % 2, y)))
    return pairs


def shrink_route():
    pairs = []
    for z, y, c, x in np.ndindex(*SIZES):
        target = device_number(z, (y // 2) * 2 + x % 2, y % 2, c * 2 + x // 2)
        pairs.append((device_number(z, y, c, x), target))
    return pairs


def back(route):
    return [(b, a) for a, b in route]


def block_ranks(block_rows):
    same = block_rows[:, :, None] == block_rows[:, None, :]
    earlier = jnp.arange(4)[None, :] < jnp.arange(4)[:, None]
    return jnp.sum(jnp.where(same & earlier[None], 1, 0), axis=2).astype(jnp.int32)


def turned(values, table, sign):
    turn, ahead, behind = table
    shape_axis = values.ndim - 1
    up = pltpu.roll(values, PAIR - ROT // 2, shape_axis)
    down = pltpu.roll(values, ROT // 2, shape_axis)
    if sign > 0:
        return values * turn + up * ahead + down * behind
    return values * turn - up * ahead - down * behind


def attention_kernel(
    seq_ref, rank_ref, limit_ref, q_ref, k_ref, v_ref, da_ref, turn_ref, ahead_ref, behind_ref,
    att_ref, dq_ref, dk_ref, dv_ref, q_low, k_low, dk_sum, dv_sum
):
    g = pl.program_id(0)
    lane = lax.broadcasted_iota(jnp.int32, (BLOCK, PAIR), 1)
    first = lane < HEAD

    def table_of(b):
        rows = pl.ds(pl.multiple_of(rank_ref[g, b] * BLOCK, BLOCK), BLOCK)
        return turn_ref[rows, :], ahead_ref[rows, :], behind_ref[rows, :]

    for b in range(4):
        rows = pl.ds(b * BLOCK, BLOCK)
        table = table_of(b)
        q_low[rows, :] = turned(q_ref[rows, :], table, 1).astype(jnp.bfloat16)
        k_low[rows, :] = turned(k_ref[rows, :], table, 1).astype(jnp.bfloat16)
    dk_sum[...] = jnp.zeros_like(dk_sum)
    dv_sum[...] = jnp.zeros_like(dv_sum)
    zero = jnp.zeros((BLOCK, PAIR), jnp.bfloat16)
    row_at = lax.broadcasted_iota(jnp.int32, (BLOCK, BLOCK), 0)
    col_at = lax.broadcasted_iota(jnp.int32, (BLOCK, BLOCK), 1)
    for b in range(4):
        rows = pl.ds(b * BLOCK, BLOCK)
        keys = pl.ds(0, (b + 1) * BLOCK)
        width = (b + 1) * BLOCK
        base = rank_ref[g, b] * BLOCK
        diagonal = (col_at <= row_at) & (col_at + base < limit_ref[g, b])
        bias_parts = []
        for e in range(b):
            away = jnp.where(seq_ref[g, e] == seq_ref[g, b], 0.0, MASKED).astype(jnp.float32)
            bias_parts.append(jnp.zeros((BLOCK, BLOCK), jnp.float32) + away)
        bias_parts.append(jnp.where(diagonal, 0.0, MASKED).astype(jnp.float32))
        bias = bias_parts[0] if b == 0 else jnp.concatenate(bias_parts, axis=1)
        q, da, k, v = q_low[rows, :], da_ref[rows, :], k_low[keys, :], v_ref[keys, :]
        qs = [jnp.where(first, q, zero), jnp.where(first, zero, q)]
        das = [jnp.where(first, da, zero), jnp.where(first, zero, da)]
        atts, probs, dss = [], [], []
        for h in range(2):
            s = dot_t(qs[h], k) * SCALE + bias
            top = jnp.max(s, axis=1, keepdims=True)
            w = jnp.exp(s - top)
            p = w * (1.0 / jnp.sum(w, axis=1, keepdims=True))
            p_low = p.astype(jnp.bfloat16)
            atts.append(dot(p_low, v))
            dp = dot_t(das[h], v)
            inner = jnp.sum(p * dp, axis=1, keepdims=True)
            dss.append((p * (dp - inner)).astype(jnp.bfloat16))
            probs.append(p_low)
        att_ref[rows, :] = jnp.where(first, atts[0], atts[1]).astype(jnp.bfloat16)
        dq = jnp.where(first, dot(dss[0], k), dot(dss[1], k)) * SCALE
        dq_ref[rows, :] = turned(dq, table_of(b), -1).astype(jnp.bfloat16)
        dk_sum[keys, :] += cross(jnp.concatenate(dss, axis=0), jnp.concatenate(qs, axis=0))
        dv_sum[keys, :] += cross(jnp.concatenate(probs, axis=0), jnp.concatenate(das, axis=0))
    for b in range(4):
        rows = pl.ds(b * BLOCK, BLOCK)
        dk_ref[rows, :] = turned(dk_sum[rows, :] * SCALE, table_of(b), -1).astype(jnp.bfloat16)
        dv_ref[rows, :] = dv_sum[rows, :].astype(jnp.bfloat16)


def attention(seq, rank, limit, queries, keys, values, d_attended):
    table = rotary_constants()
    whole = pl.BlockSpec((GROUP, PAIR), lambda g, p: (0, 0))
    part = pl.BlockSpec((GROUP, PAIR), lambda g, p: (g, p))
    smem = pl.BlockSpec(memory_space=pltpu.SMEM)
    rows = queries.shape[0]
    out = jax.ShapeDtypeStruct((rows, 2 * PAIR), jnp.bfloat16)
    return pl.pallas_call(
        attention_kernel,
        grid=(rows // GROUP, 2),
        in_specs=[smem, smem, smem, part, part, part, part, whole, whole, whole],
        out_specs=[part] * 4,
        out_shape=[out] * 4,
        scratch_shapes=[
            pltpu.VMEM((GROUP, PAIR), jnp.bfloat16),
            pltpu.VMEM((GROUP, PAIR), jnp.bfloat16),
            pltpu.VMEM((GROUP, PAIR), jnp.float32),
            pltpu.VMEM((GROUP, PAIR), jnp.float32),
        ],
        compiler_params=pltpu.CompilerParams(vmem_limit_bytes=32 * 2**20),
        cost_estimate=pl.CostEstimate(
            flops=2_000_000_000, bytes_accessed=6 * 2**20, transcendentals=2_000_000
        ),
        name="attention",
    )(seq, rank, limit, queries, keys, values, d_attended, *(jnp.asarray(a) for a in table))


def adam_step(weight, moment, second, gradient, step_rate, step_decay):
    moment_new = BETA_ONE * moment + (1 - BETA_ONE) * gradient
    second_new = BETA_TWO * second + (1 - BETA_TWO) * gradient * gradient
    moment_hat = moment_new / (1 - BETA_ONE**STEP)
    second_hat = second_new / (1 - BETA_TWO**STEP)
    updated = weight - step_rate * (
        moment_hat / (jnp.sqrt(second_hat) + ADAM_EPS) + step_decay * weight
    )
    return (second_new, updated)


def columns_out(value, chunks):
    rows = value.shape[0]
    parts = value.reshape(rows, chunks, TPN, PAIR).transpose(2, 0, 1, 3)
    parts = parts.reshape(TPN, rows, chunks * PAIR)
    return lax.all_to_all(parts, TP, split_axis=0, concat_axis=0, tiled=True).reshape(
        TPN * rows, chunks * PAIR
    )


def columns_back(value, chunks):
    rows = value.shape[0] // TPN
    parts = value.reshape(TPN, rows, chunks * PAIR)
    parts = lax.all_to_all(parts, TP, split_axis=0, concat_axis=0, tiled=True)
    parts = parts.reshape(TPN, rows, chunks, PAIR).transpose(1, 2, 0, 3)
    return parts.reshape(rows, chunks * TPN * PAIR)


def own_columns(vector, chunks, t):
    parts = vector.reshape(chunks, TPN, PAIR)
    return lax.dynamic_index_in_dim(parts, t, axis=1, keepdims=False).reshape(chunks * PAIR)


def spread_columns(vector, chunks, t):
    parts = jnp.zeros((chunks, TPN, PAIR), jnp.float32)
    parts = lax.dynamic_update_index_in_dim(parts, vector.reshape(chunks, PAIR), t, axis=1)
    return parts.reshape(-1)


def gathered(value, axes):
    return lax.all_gather(value, axes, axis=0, tiled=True)


def summed(value, axes):
    return lax.psum_scatter(value, axes, scatter_dimension=0, tiled=True)


def shards(
    tokens, cotangent, block_seq, seq_lengths,
    qkv_weight, qkv_moment, qkv_second,
    dense_weight, dense_moment, dense_second,
    expand_weight, expand_moment, expand_second,
    shrink_weight, shrink_moment, shrink_second,
    vectors, vec_moment, vec_second,
):
    t = lax.axis_index("c") * 4 + lax.axis_index("x")
    low = jnp.bfloat16
    vec_all = gathered(vectors.astype(low), ALL).astype(jnp.float32)
    expand_cols = columns_out(expand_weight.astype(low), 8)
    qkv_cols = columns_out(qkv_weight.astype(low), 6)
    dense_rows = lax.ppermute(dense_weight.astype(low), ALL, dense_route())
    shrink_rows = lax.ppermute(shrink_weight.astype(low), ALL, shrink_route())
    w_expand = gathered(expand_cols, ZY)
    w_qkv = gathered(qkv_cols, ZY)
    w_dense = gathered(dense_rows, ZY)
    w_shrink = gathered(shrink_rows, ZY)

    norm_gain, norm_shift = vec_all[:MODEL], vec_all[MODEL : 2 * MODEL]
    bias_qkv = own_columns(vec_all[2 * MODEL : 5 * MODEL], 6, t)
    bias_dense = vec_all[5 * MODEL : 6 * MODEL]
    bias_expand = own_columns(vec_all[6 * MODEL : 6 * MODEL + FF], 8, t)
    bias_shrink = vec_all[6 * MODEL + FF :]

    block_rows = gathered(block_seq, "c")
    length_rows = gathered(seq_lengths, "c")
    ranks = block_ranks(block_rows)
    limits = jnp.where(block_rows == 0, length_rows[:, :1], length_rows[:, 1:])

    c, x = lax.axis_index("c"), lax.axis_index("x")
    my_rank = lax.dynamic_index_in_dim(ranks[c], x, keepdims=False)
    my_limit = lax.dynamic_index_in_dim(limits[c], x, keepdims=False)
    live = my_rank * BLOCK + jnp.arange(BLOCK, dtype=jnp.int32) < my_limit

    inputs = tokens.astype(jnp.float32)
    mean = jnp.mean(inputs, axis=1, keepdims=True)
    center = inputs - mean
    inverse = lax.rsqrt(jnp.mean(center * center, axis=1, keepdims=True) + NORM_EPS)
    xhat = center * inverse
    normed_own = (xhat * norm_gain + norm_shift).astype(low)
    d_out_own = jnp.where(live[:, None], cotangent, jnp.zeros_like(cotangent))
    normed = gathered(normed_own, TP)
    d_out = gathered(d_out_own, TP)

    pre = dot(normed, w_expand) + bias_expand
    inner = jnp.tanh(GELU_A * (pre + GELU_B * (pre * pre * pre)))
    act = (0.5 * pre * (1.0 + inner)).astype(low)
    slope = 0.5 * (1.0 + inner) + 0.5 * pre * (1.0 - inner * inner) * (
        GELU_A * (1.0 + 3.0 * GELU_B * (pre * pre))
    )
    shrink_sum = summed(cross(act, d_out).astype(low), ZY)

    projected = dot(normed, w_qkv) + bias_qkv
    d_attended = dot_t(d_out, w_dense).astype(low)
    attended, d_q, d_k, d_v = attention(
        block_rows, ranks, limits,
        projected[:, : 2 * PAIR],
        projected[:, 2 * PAIR : 4 * PAIR],
        projected[:, 4 * PAIR :].astype(low),
        d_attended,
    )
    dense_sum = summed(cross(attended, d_out).astype(low), ZY)
    d_qkv = jnp.concatenate([d_q, d_k, d_v], axis=1)
    qkv_sum = summed(cross(normed, d_qkv).astype(low), ZY)
    d_pre = (dot_t(d_out, w_shrink) * slope).astype(low)
    expand_sum = summed(cross(normed, d_pre).astype(low), ZY)

    branches = summed((dot(attended, w_dense) + dot(act, w_shrink)).astype(low), TP)
    output = (inputs + (branches.astype(jnp.float32) + (bias_dense + bias_shrink))).astype(low)

    d_normed = summed((dot_t(d_qkv, w_qkv) + dot_t(d_pre, w_expand)).astype(low), TP)
    d_normed = d_normed.astype(jnp.float32)
    e = d_normed * norm_gain
    d_inputs = inverse * (
        e
        - jnp.mean(e, axis=1, keepdims=True)
        - xhat * jnp.mean(e * xhat, axis=1, keepdims=True)
    )
    input_grad = (d_out_own.astype(jnp.float32) + d_inputs).astype(low)

    d_out_sum = jnp.sum(d_out_own, axis=0, dtype=jnp.float32)
    vec_terms = jnp.concatenate(
        [
            jnp.sum(d_normed * xhat, axis=0),
            jnp.sum(d_normed, axis=0),
            spread_columns(jnp.sum(d_qkv, axis=0, dtype=jnp.float32), 6, t),
            d_out_sum,
            spread_columns(jnp.sum(d_pre, axis=0, dtype=jnp.float32), 8, t),
            d_out_sum,
        ]
    )
    vec_grad = summed(vec_terms, ALL)

    shrink_grad = lax.ppermute(shrink_sum, ALL, back(shrink_route())).astype(jnp.float32)
    dense_grad = lax.ppermute(dense_sum, ALL, back(dense_route())).astype(jnp.float32)
    qkv_grad = columns_back(qkv_sum, 6).astype(jnp.float32)
    expand_grad = columns_back(expand_sum, 8).astype(jnp.float32)

    masters = (qkv_weight, dense_weight, expand_weight, shrink_weight, vectors)
    moments = (qkv_moment, dense_moment, expand_moment, shrink_moment, vec_moment)
    seconds = (qkv_second, dense_second, expand_second, shrink_second, vec_second)
    gradients = (qkv_grad, dense_grad, expand_grad, shrink_grad, vec_grad)
    results = [output, input_grad]
    for i in range(5):
        state_new, weight_new = adam_step(
            masters[i], moments[i], seconds[i], gradients[i], RATES[i], DECAYS[i]
        )
        results.extend([gradients[i], state_new, weight_new])
    return tuple(results)


def solution(mesh):
    finer = Mesh(mesh.devices.reshape(*SIZES), ALL)
    whole, group = P(ALL, None), P(DP, None)
    return jax.shard_map(
        shards,
        mesh=finer,
        in_specs=(whole, whole, group, group, *[whole] * 12, *[P(ALL)] * 3),
        out_specs=(*[whole] * 14, *[P(ALL)] * 3),
        check_vma=False,
    )
```

time: 1150 us -> 945 us (0.82)
  local copies, waits for them, and re-layouts: 176 us -> 14 us
  matrix products: 196 us -> 82 us
  waiting for transfers between devices: 554 us -> 655 us
  other arithmetic: 97.5 us -> 22.6 us
  starting transfers between devices: 5.9 us -> 33.2 us
  Pallas kernels: 0 us -> 18.5 us
    unnamed x10 -> x14, waiting for transfers between devices: 0.15 us -> 141 us
    dot_general x18 -> x12, matrix products: 196 us -> 82 us  [the longest x4 27.9 us: dot(): return jnp.dot(a, b, preferred_element_type=jnp.float32)]
    reshape x6 -> x4, local copies, waits for them, and re-layouts: 111 us -> 0.45 us  [the longest x2 0.36 us: columns_out(): parts = parts.reshape(TPN, rows, chunks * PAIR)]
    concatenate x4 -> x0, other arithmetic: 67.6 us -> none  [the longest x1 65.7 us: shards(): jnp.concatenate([qkv_term, dense_term, expand_term, shrink_term], axis=1)]
    reduce_scatter x3 -> x6, waiting for transfers between devices: 363 us -> 325 us  [summed(): return lax.psum_scatter(value, axes, scatter_dimension=0, tiled=True)]
    slice x12 -> x6, local copies, waits for them, and re-layouts: 28.9 us -> 1.16 us  [the longest x1 0.85 us: shards(): projected[:, 4 * PAIR:].astype(low)]
    unnamed x3 -> x1, blocking collectives: 93.1 us -> 69.3 us
    all_to_all x0 -> x2, blocking collectives: none -> 21.3 us  [columns_out(): lax.all_to_all(parts, TP, split_axis=0, concat_axis=0, tiled=True)]
  transfers between devices with their start and end apart: 9 -> 19, of which waited for: 5 -> 17; matrix products, arithmetic and copies ran while one was open for 29% -> 10% of each run, Pallas kernels for 0% -> 2%
where the time goes in v1:
time: 945 us; the launch traced here: 935 us
  waiting for transfers between devices  655 us (69%)
  blocking collectives  94.1 us (10%)
  matrix products  82 us (9%)
  starting transfers between devices  33.2 us (4%)
  other arithmetic  22.6 us (2%)
  Pallas kernels  18.5 us (2%)
  between operations  15.7 us (2%)
  local copies, waits for them, and re-layouts  14 us (1%)
    reduce_scatter x6, waiting for transfers between devices, summed(): return lax.psum_scatter(value, axes, scatter_dimension=0, tiled=True)  325 us
    all_gather x6, waiting for transfers between devices, gathered(): return lax.all_gather(value, axes, axis=0, tiled=True)  169 us
    unnamed x14, waiting for transfers between devices  141 us
    unnamed x1, blocking collectives  69.3 us
    dot_general x4, matrix products, dot(): return jnp.dot(a, b, preferred_element_type=jnp.float32)  27.9 us
    dot_general x4, matrix products, dot_t(): lax.dot_general(a, b, (((1,), (1,)), ((), ())), preferred_element_type=jn...  27.6 us
    dot_general x4, matrix products, cross(): lax.dot_general(a, b, (((0,), (0,)), ((), ())), preferred_element_type=jn...  26.6 us
    all_to_all x2, blocking collectives, columns_out(): lax.all_to_all(parts, TP, split_axis=0, concat_axis=0, tiled=True)  21.3 us
  transfers between devices with their start and end apart: 19, of which 17 were waited for; matrix products, arithmetic and copies ran while one was open for 10% of the time, Pallas kernels for 2%

profile of v1, /device:TPU:1, one launch (start us, length us, event | category | flops | bytes accessed | tf_op | source)
XLA Modules:
  0.0 935.3 jit_solution(13381002829691763456)
XLA Ops:
  10.8 69.3 %all-reduce = bf16[22528]{0:T(1024)(128)(2,1)S(1)} all-reduce(bf16[22528]{0:T(1024)(128)(2,1)S(1)} %dynamic-update-slice), channel_id=1, replica_groups=mesh['z'=4,'y'=4,'c'=2,'x'=4] {'z','y','c','x'}, use_global_device_ids=true, to_apply=%add | all-reduce | flops 22528 | bytes 90112
  83.7 12.1 %all_to_all.20 = bf16[8,16,1024]{2,1,0:T(8,128)(2,1)} all-to-all(bf16[8,16,1024]{2,1,0:T(8,128)(2,1)S(1)} %reshape.154), channel_id=1, replica_groups=mesh['z'=4,'y'=4,'c'=2,'x'=4] {'c','x'}, dimensions={0} | all-to-all | bytes 524288 | tf_op jit(solution)/shard_map/all_to_all | solution.py:206
  104.2 8.8 all-gather.9.cloned.1.call-done
  113.0 51.8 %all-gather.17.cloned.1.call-done = bf16[2048,1024]{1,0:T(8,128)(2,1)} async-done(((bf16[128,1024]{1,0:T(8,128)(2,1)}), bf16[2048,1024]{1,0:T(8,128)(2,1)}) %all-gather.17.cloned.1.call-update) | async-done | bytes 4194320 | tf_op jit(solution)/shard_map/all_gather | solution.py:231
  164.8 9.9 %fusion.39 = f32[1024,1024]{1,0:T(8,128)} fusion(bf16[1024,2048]{1,0:T(8,128)(2,1)} %all-gather.9.cloned.1.call-done, bf16[2048,1024]{1,0:T(8,128)(2,1)} %all-gather.17.cloned.1.call-done), kind=kOutput, calls=%fused_computation.97 | convolution fusion | flops 4294967296 | bytes 12582912 | tf_op jit(solution)/shard_map/dot_general | solution.py:40
  174.8 24.5 %all-gather.13.cloned.1.call-done = bf16[1024,2048]{1,0:T(8,128)(2,1)} async-done(((bf16[128,2048]{1,0:T(8,128)(2,1)}), bf16[1024,2048]{1,0:T(8,128)(2,1)}) %all-gather.13.cloned.1.call-update) | async-done | bytes 4194320 | tf_op jit(solution)/shard_map/all_gather | solution.py:231
  199.2 10.7 %convolution_convert_fusion = bf16[1024,2048]{1,0:T(8,128)(2,1)} fusion(bf16[1024,2048]{1,0:T(8,128)(2,1)} %all-gather.13.cloned.1.call-done, f32[1024,1024]{1,0:T(8,128)} %fusion.39, f32[1024]{0:T(1024)S(1)} %bitcast.93), kind=kOutput, calls=%fused_computation.16 | convolution fusion | flops 4307550208 | bytes 12587008 | tf_op jit(solution)/shard_map/dot_general | solution.py:48
  211.3 9.2 all_to_all.21
  228.2 59.0 %reduce-scatter.17.cloned.1.call-done = bf16[64,2048]{1,0:T(8,128)(2,1)} async-done(((bf16[1024,2048]{1,0:T(8,128)(2,1)}), bf16[64,2048]{1,0:T(8,128)(2,1)}) %reduce-scatter.17.cloned.1.call-update) | async-done | bytes 262160 | tf_op jit(solution)/shard_map/reduce_scatter | solution.py:235
  292.2 7.3 collective-permute-done.3
  310.8 28.0 %all-gather.11.cloned.1.call-done = bf16[2048,768]{1,0:T(8,128)(2,1)} async-done(((bf16[128,768]{1,0:T(8,128)(2,1)}), bf16[2048,768]{1,0:T(8,128)(2,1)}) %all-gather.11.cloned.1.call-update) | async-done | bytes 3145744 | tf_op jit(solution)/shard_map/all_gather | solution.py:231
  346.1 36.1 %all-gather.15.cloned.1.call-done = bf16[256,2048]{1,0:T(8,128)(2,1)} async-done(((bf16[16,2048]{1,0:T(8,128)(2,1)}), bf16[256,2048]{1,0:T(8,128)(2,1)}) %all-gather.15.cloned.1.call-update) | async-done | bytes 1048592 | tf_op jit(solution)/shard_map/all_gather | solution.py:231
  386.1 18.5 %attention.1 = (bf16[1024,256]{1,0:T(8,128)(2,1)S(1)}, bf16[1024,256]{1,0:T(8,128)(2,1)S(1)}, bf16[1024,256]{1,0:T(8,128)(2,1)S(1)}, bf16[1024,256]{1,0:T(8,128)(2,1)S(1)}) custom-call(s32[2,4]{1,0:T(2,128)S(1)} %bitcast.78, s32[2,4]{1,0:T(2,128)S(1)} %select_reduce_fusion.rank_ref, s32[2,4]{1,0:T(2,128)S(1)} %compare_select_fusion.limit_ref, ...), custom_call_target="tpu_custom_call" | custom-call | flops 2000000000 | bytes 6291456 | tf_op jit(solution)/shard_map/attention/pallas_call | solution.py:171
  409.8 7.4 convolution_convert_fusion.2
  417.5 20.0 %all-gather.19.cloned.1.call-done = bf16[1024,2048]{1,0:T(8,128)(2,1)} async-done(((bf16[64,2048]{1,0:T(8,128)(2,1)}), bf16[1024,2048]{1,0:T(8,128)(2,1)}) %all-gather.19.cloned.1.call-update) | async-done | bytes 4194320 | tf_op jit(solution)/shard_map/all_gather | solution.py:231
  437.5 12.0 %convert_reduce_fusion = (f32[1024]{0:T(1024)}, bf16[1024,1024]{1,0:T(8,128)(2,1)S(1)}) fusion(f32[1024,1024]{1,0:T(8,128)} %fusion.39, f32[1024]{0:T(1024)S(1)} %bitcast.94, bf16[1024,2048]{1,0:T(8,128)(2,1)} %all-gather.13.cloned.1.call-done, bf16[1024,2048]{1,0:T(8,128)(2,1)} %all-gather.19.cloned.1.call-done), kind=kOutput, calls=%fused_computation.14 | convolution fusion | flops 4316986368 | bytes 14688256 | tf_op jit(solution)/shard_map/dot_general | solution.py:44
  470.6 8.4 fusion.31
  483.9 28.3 %reduce-scatter.13.cloned.1.call-done = bf16[16,2048]{1,0:T(8,128)(2,1)} async-done(((bf16[256,2048]{1,0:T(8,128)(2,1)}), bf16[16,2048]{1,0:T(8,128)(2,1)}) %reduce-scatter.13.cloned.1.call-update) | async-done | bytes 65552 | tf_op jit(solution)/shard_map/reduce_scatter | solution.py:235
  517.5 73.2 %reduce-scatter.11.cloned.1.call-done = bf16[128,768]{1,0:T(8,128)(2,1)} async-done(((bf16[2048,768]{1,0:T(8,128)(2,1)}), bf16[128,768]{1,0:T(8,128)(2,1)}) %reduce-scatter.11.cloned.1.call-update) | async-done | bytes 196624 | tf_op jit(solution)/shard_map/reduce_scatter | solution.py:235
  606.7 64.3 %reduce-scatter.15.cloned.1.call-done = bf16[128,1024]{1,0:T(8,128)(2,1)} async-done(((bf16[2048,1024]{1,0:T(8,128)(2,1)}), bf16[128,1024]{1,0:T(8,128)(2,1)}) %reduce-scatter.15.cloned.1.call-update) | async-done | bytes 262160 | tf_op jit(solution)/shard_map/reduce_scatter | solution.py:235
  671.0 6.5 all-to-all-start.3
  677.6 49.0 %reduce-scatter.9.cloned.1.call-done = bf16[128,2048]{1,0:T(8,128)(2,1)} async-done(((bf16[1024,2048]{1,0:T(8,128)(2,1)}), bf16[128,2048]{1,0:T(8,128)(2,1)}) %reduce-scatter.9.cloned.1.call-update) | async-done | bytes 524304 | tf_op jit(solution)/shard_map/reduce_scatter | solution.py:235
  729.6 51.3 %reduce-scatter.7.cloned.1.call-done = bf16[128,2048]{1,0:T(8,128)(2,1)} async-done(((bf16[1024,2048]{1,0:T(8,128)(2,1)}), bf16[128,2048]{1,0:T(8,128)(2,1)}) %reduce-scatter.7.cloned.1.call-update) | async-done | bytes 524304 | tf_op jit(solution)/shard_map/reduce_scatter | solution.py:235
  783.7 141.2 %all-reduce.4.cloned.1.call-done = f32[22528]{0:T(1024)} async-done(((f32[22528]{0:T(1024)}), f32[22528]{0:T(1024)}) %all-reduce.4.cloned.1.call-update) | async-done | bytes 90128
  (192 shorter events, 112.8 us)
Async XLA Ops:
  7.2 105.8 %all-gather.9.cloned.1.call-start = ((), (), s32[]{:S(2)}) async-start(), calls=%async_computation.10 | async-start | bytes 4718592 | tf_op jit(solution)/shard_map/all_gather | solution.py:231
  82.4 82.5 %all-gather.17.cloned.1.call-start = ((), (), s32[]{:S(2)}) async-start(), calls=%async_computation.14 | async-start | bytes 4456448 | tf_op jit(solution)/shard_map/all_gather | solution.py:231
  95.9 103.4 %all-gather.13.cloned.1.call-start = ((), (), s32[]{:S(2)}) async-start(), calls=%async_computation.12 | async-start | bytes 4718592 | tf_op jit(solution)/shard_map/all_gather | solution.py:231
  104.1 183.1 %reduce-scatter.17.cloned.1.call-start = ((), (), s32[]{:S(2)}) async-start(), calls=%async_computation.21 | async-start | bytes 4456448 | tf_op jit(solution)/shard_map/reduce_scatter | solution.py:235
  209.9 128.9 %all-gather.11.cloned.1.call-start = ((), (), s32[]{:S(2)}) async-start(), calls=%async_computation.11 | async-start | bytes 3342336 | tf_op jit(solution)/shard_map/all_gather | solution.py:231
  220.5 161.7 %all-gather.15.cloned.1.call-start = ((), (), s32[]{:S(2)}) async-start(), calls=%async_computation.13 | async-start | bytes 1114112 | tf_op jit(solution)/shard_map/all_gather | solution.py:231
  220.7 6.8 collective-permute-start
  228.2 209.3 %all-gather.19.cloned.1.call-start = ((), (), s32[]{:S(2)}) async-start(), calls=%async_computation.15 | async-start | bytes 4456448 | tf_op jit(solution)/shard_map/all_gather | solution.py:231
  287.2 12.3 %collective-permute-start.3 = (bf16[64,2048]{1,0:T(8,128)(2,1)}, bf16[64,2048]{1,0:T(8,128)(2,1)S(1)}, u32[]{:S(2)}, u32[]{:S(2)}) collective-permute-start(bf16[64,2048]{1,0:T(8,128)(2,1)} %reduce-scatter.17.cloned.1.call-done), channel_id=1, source_target_pairs={{0,0},{8,1},{1,2},{9,3},{2,4},{10,5},{3,6},{11,7},{4,8},{12,9},{5,... | collective-permute-start | bytes 786440 | tf_op jit(solution)/shard_map/ppermute | solution.py:333
  300.8 9.2 collective-permute-start.1
  310.7 201.5 %reduce-scatter.13.cloned.1.call-start = ((), (), s32[]{:S(2)}) async-start(), calls=%async_computation.19 | async-start | bytes 1114112 | tf_op jit(solution)/shard_map/reduce_scatter | solution.py:235
  408.5 182.3 %reduce-scatter.11.cloned.1.call-start = ((), (), s32[]{:S(2)}) async-start(), calls=%async_computation.18 | async-start | bytes 3342336 | tf_op jit(solution)/shard_map/reduce_scatter | solution.py:235
  417.2 253.8 %reduce-scatter.15.cloned.1.call-start = ((), (), s32[]{:S(2)}) async-start(), calls=%async_computation.20 | async-start | bytes 4456448 | tf_op jit(solution)/shard_map/reduce_scatter | solution.py:235
  457.2 269.4 %reduce-scatter.9.cloned.1.call-start = ((), (), s32[]{:S(2)}) async-start(), calls=%async_computation.17 | async-start | bytes 4718592 | tf_op jit(solution)/shard_map/reduce_scatter | solution.py:235
  470.3 310.5 %reduce-scatter.7.cloned.1.call-start = ((), (), s32[]{:S(2)}) async-start(), calls=%async_computation.16 | async-start | bytes 4718592 | tf_op jit(solution)/shard_map/reduce_scatter | solution.py:235
  483.9 245.0 %copy-start.32 = (f32[2048]{0:T(1024)S(1)}, f32[2048]{0:T(1024)}, u32[]{:S(2)}) copy-start(f32[2048]{0:T(1024)} %get-tuple-element.34) | copy-start | bytes 24580
  512.2 85.1 %collective-permute-start.2 = (bf16[16,2048]{1,0:T(8,128)(2,1)}, bf16[16,2048]{1,0:T(8,128)(2,1)S(1)}, u32[]{:S(2)}, u32[]{:S(2)}) collective-permute-start(bf16[16,2048]{1,0:T(8,128)(2,1)} %reduce-scatter.13.cloned.1.call-done), channel_id=1, source_target_pairs={{0,0},{8,1},{16,2},{24,3},{32,4},{40,5},{48,6},{56,7},{1,8},{9,9},... | collective-permute-start | bytes 196616 | tf_op jit(solution)/shard_map/ppermute | solution.py:334
  517.5 263.4 %copy-start.9 = (bf16[128,2048]{1,0:T(8,128)(2,1)S(1)}, bf16[128,2048]{1,0:T(8,128)(2,1)}, u32[]{:S(2)}) copy-start(bf16[128,2048]{1,0:T(8,128)(2,1)} %get-tuple-element.35) | copy-start | bytes 1572868
  590.7 12.4 %all-to-all-start.2 = ((bf16[8,16,768]{2,1,0:T(8,128)(2,1)}), bf16[8,16,768]{2,1,0:T(8,128)(2,1)S(1)}, u32[]{:S(2)}, u32[]{:S(2)}) async-start(bf16[8,16,768]{2,1,0:T(8,128)(2,1)} %bitcast.91), calls=%async_computation.5 | async-start | bytes 393216 | tf_op jit(solution)/shard_map/all_to_all | solution.py:214
  603.6 323.1 %copy-start.12 = (f32[16,8192]{1,0:T(8,128)S(1)}, f32[16,8192]{1,0:T(8,128)}, u32[]{:S(2)}) copy-start(f32[16,8192]{1,0:T(8,128)} %param.32) | copy-start | bytes 1572868
  603.7 323.1 %copy-start.19 = (f32[16,8192]{1,0:T(8,128)S(1)}, f32[16,8192]{1,0:T(8,128)}, u32[]{:S(2)}) copy-start(f32[16,8192]{1,0:T(8,128)} %param.33) | copy-start | bytes 1572868
  603.7 323.1 %copy-start.20 = (f32[16,8192]{1,0:T(8,128)S(1)}, f32[16,8192]{1,0:T(8,128)}, u32[]{:S(2)}) copy-start(f32[16,8192]{1,0:T(8,128)} %param.34) | copy-start | bytes 1572868
  671.0 255.3 %all-to-all-start.3 = ((bf16[8,16,1024]{2,1,0:T(8,128)(2,1)}), bf16[8,16,1024]{2,1,0:T(8,128)(2,1)S(1)}, u32[]{:S(2)}, u32[]{:S(2)}) async-start(bf16[8,16,1024]{2,1,0:T(8,128)(2,1)} %bitcast.90), calls=%async_computation.8 | async-start | bytes 524288 | tf_op jit(solution)/shard_map/all_to_all | solution.py:214
  677.6 247.4 %all-reduce.4.cloned.1.call-start = ((), (), s32[]{:S(2)}) async-start(), calls=%async_computation.22 | async-start | bytes 180224
  (38 other events, 2349.9 us)
Sparse Core Ops, SparseCore 0:
  82.5 30.4 all-gather.8
  115.2 49.6 all-gather.16
  167.1 32.0 all-gather.12
  210.1 77.0 reduce-scatter.16
  289.4 49.3 all-gather.10
  341.6 40.4 all-gather.14
  385.1 52.3 all-gather.18
  441.0 71.0 reduce-scatter.12
  515.5 75.1 reduce-scatter.10
  593.9 77.0 reduce-scatter.14
  673.5 52.9 reduce-scatter.8
  729.0 51.8 reduce-scatter.6
  786.9 138.0 all-reduce.3

commit v2 on v1

--- a/solution.py
+++ b/solution.py
@@ -23,6 +23,7 @@
 TP = ("c", "x")
 SIZES = (4, 4, 2, 4)
 TPN = 8
+COPIES = 128
 SCALE = HEAD ** (-0.5)
 
 NORM_EPS = 1e-05
@@ -62,27 +63,250 @@
     return tuple(np.concatenate([a, a], axis=1) for a in (turn, ahead, behind))
 
 
-def device_number(z, y, c, x):
-    return ((z * 4 + y) * 2 + c) * 4 + x
-
-
-def dense_route():
-    pairs = []
-    for z, y, c, x in np.ndindex(*SIZES):
-        pairs.append((device_number(z, y, c, x), device_number((z // 2) * 2 + c, x, z % 2, y)))
-    return pairs
-
-
-def shrink_route():
-    pairs = []
-    for z, y, c, x in np.ndindex(*SIZES):
-        target = device_number(z, (y // 2) * 2 + x % 2, y % 2, c * 2 + x // 2)
-        pairs.append((device_number(z, y, c, x), target))
-    return pairs
-
-
-def back(route):
-    return [(b, a) for a, b in route]
+MESH = pl.DeviceIdType.MESH
+
+
+def other(axis, step):
+    size = SIZES[ALL.index(axis)]
+    return lax.rem(lax.axis_index(axis) + step + size, size)
+
+
+class Copies:
+    def __init__(self, send, recv):
+        self.send, self.recv, self.count, self.open = send, recv, 0, []
+
+    def start(self, src, dst, to):
+        at = self.count
+        self.count += 1
+        copy = pltpu.make_async_remote_copy(
+            src_ref=src,
+            dst_ref=dst,
+            send_sem=self.send.at[at],
+            recv_sem=self.recv.at[at],
+            device_id=to,
+            device_id_type=MESH,
+        )
+        copy.start()
+        self.open.append(copy)
+        return copy
+
+    def finish(self):
+        for copy in self.open:
+            copy.wait_send()
+        self.open = []
+
+
+def enter():
+    barrier = pltpu.get_barrier_semaphore()
+    for partner in token_partners() + weight_partners() + [dense_partner()]:
+        pl.semaphore_signal(barrier, inc=1, device_id=partner, device_id_type=MESH)
+    pl.semaphore_wait(barrier, 23)
+
+
+def token_partners():
+    return [{"c": other("c", i), "x": other("x", j)} for i in range(2) for j in range(4) if i + j]
+
+
+def weight_partners():
+    return [{"z": other("z", i), "y": other("y", j)} for i in range(4) for j in range(4) if i + j]
+
+
+def dense_partner():
+    z, y, c, x = (lax.axis_index(a) for a in ALL)
+    return {"z": (1 - z // 2) * 2 + c, "y": x, "c": lax.rem(z, 2), "x": y}
+
+
+def gather_weights(copies, view):
+    z, y = lax.axis_index("z"), lax.axis_index("y")
+    up, down = {"y": other("y", 1)}, {"y": other("y", -1)}
+    far, near = {"z": other("z", 1)}, {"z": other("z", -1)}
+    every = slice(None)
+
+    def go(block, to):
+        return copies.start(block, block, to)
+
+    a_up, a_down = go(view(z, y, 4), up), go(view(z, y, 4), down)
+    b_far, b_near = go(view(z, y, 5), far), go(view(z, y, 5), near)
+    yield
+    a_up.wait_recv()
+    a_up = go(view(z, other("y", -1), 0), up)
+    b_far.wait_recv()
+    b_far = go(view(other("z", -1), y, 2), far)
+    a_down.wait_recv()
+    a_down = go(view(z, other("y", 1), 1), down)
+    b_near.wait_recv()
+    b_near = go(view(other("z", 1), y, 3), near)
+    yield
+    a_up.wait_recv()
+    a_down.wait_recv()
+    a_far, a_near = go(view(z, every, 4), far), go(view(z, every, 4), near)
+    b_far.wait_recv()
+    b_near.wait_recv()
+    b_up, b_down = go(view(every, y, 5), up), go(view(every, y, 5), down)
+    yield
+    a_far.wait_recv()
+    a_far = go(view(other("z", -1), every, 0), far)
+    b_up.wait_recv()
+    b_up = go(view(every, other("y", -1), 2), up)
+    a_near.wait_recv()
+    a_near = go(view(other("z", 1), every, 1), near)
+    b_down.wait_recv()
+    b_down = go(view(every, other("y", 1), 3), down)
+    yield
+    for copy in (a_far, a_near, b_up, b_down):
+        copy.wait_recv()
+
+
+def gather_tokens(copies, ref):
+    c, x, across = lax.axis_index("c"), lax.axis_index("x"), other("c", 1)
+
+    def go(block, to):
+        return copies.start(block, block, to)
+
+    own = ref.at[c, x]
+    right, left, core = go(own, {"x": other("x", 1)}), go(own, {"x": other("x", -1)}), [go(own, {"c": across})]
+    yield
+    right.wait_recv()
+    came = ref.at[c, other("x", -1)]
+    right = go(ref.at[c, other("x", -1), pl.ds(0, 64)], {"x": other("x", 1)})
+    core.append(go(came, {"c": across}))
+    left.wait_recv()
+    came = ref.at[c, other("x", 1)]
+    left = go(ref.at[c, other("x", 1), pl.ds(64, 64)], {"x": other("x", -1)})
+    core.append(go(came, {"c": across}))
+    yield
+    right.wait_recv()
+    left.wait_recv()
+    core.append(go(ref.at[c, other("x", 2)], {"c": across}))
+    yield
+    for copy in core:
+        copy.wait_recv()
+
+
+def gather_vectors(copies, ref):
+    z, y, c, x = (lax.axis_index(a) for a in ALL)
+    sent = [copies.start(ref.at[z, y, c, x], ref.at[z, y, c, x], to) for to in token_partners()]
+    yield
+    for copy in sent:
+        copy.wait_recv()
+    sent = [copies.start(ref.at[z, y], ref.at[z, y], to) for to in weight_partners()]
+    yield
+    for copy in sent:
+        copy.wait_recv()
+
+
+def expand_to_group(copies, send, ref, width):
+    z, y, c, x = (lax.axis_index(a) for a in ALL)
+    rows = pl.ds(pl.multiple_of((c * 4 + x) * 16, 16), 16)
+    sent = []
+    for to in token_partners():
+        sent.append(copies.start(send.at[to["c"] * 4 + to["x"]], ref.at[z, y, rows], to))
+    ref[z, y, rows] = send[c * 4 + x]
+    yield
+    for copy in sent:
+        copy.wait_recv()
+
+
+def by_rows(ref, rows):
+    quarter = rows // 4
+
+    def view(z, y, part):
+        start, size = (part * quarter, quarter) if part < 4 else ((part - 4) * 2 * quarter, 2 * quarter)
+        return ref.at[z, y, pl.ds(start, size)]
+
+    return view
+
+
+def by_columns(ref, columns):
+    quarter = columns // 4
+
+    def view(z, y, part):
+        start, size = (part * quarter, quarter) if part < 4 else ((part - 4) * 2 * quarter, 2 * quarter)
+        return ref.at[z, y, :, pl.ds(start, size)]
+
+    return view
+
+
+def step(*works):
+    for work in works:
+        next(work, None)
+
+
+def row_of(ref, first, count):
+    return jnp.concatenate([ref[pl.ds(first + i, 1), :] for i in range(count)], axis=1)
+
+
+def gather_kernel(
+    tokens_ref, d_out_ref, we_send, wq_send, wd_own, ws_own, vec_own,
+    we, wq, wd, ws, normed, d_out, vec_rows, vec_all, send, recv,
+):
+    z, y, c, x = (lax.axis_index(a) for a in ALL)
+    copies = Copies(send, recv)
+    ws[z, y] = ws_own[...]
+    vec_all[z, y, c, x] = vec_own[...]
+    d_out[c, x] = d_out_ref[...]
+    enter()
+    vectors = gather_vectors(copies, vec_all)
+    step(vectors)
+    shrink = gather_weights(copies, by_rows(ws, 64))
+    step(shrink)
+    into_expand = expand_to_group(copies, we_send, we, 1024)
+    step(into_expand)
+    dense_here = copies.start(wd_own, wd.at[dense_partner()["z"], dense_partner()["y"]], dense_partner())
+    into_qkv = expand_to_group(copies, wq_send, wq, 768)
+    step(into_qkv)
+    cotangent = gather_tokens(copies, d_out)
+    step(cotangent)
+    step(vectors)
+    step(into_expand)
+    expand = gather_weights(copies, by_rows(we, 128))
+    step(expand)
+    step(vectors)
+    vec_rows[...] = jnp.zeros_like(vec_rows)
+    for d in range(128):
+        first = (176 * d) // 128
+        vec_rows[pl.ds(first, 3), :] += vec_all[d // 32, (d // 8) % 4, (d // 4) % 2, d % 4, pl.ds(0, 3), :]
+    values = tokens_ref[...].astype(jnp.float32)
+    center = values - jnp.mean(values, axis=1, keepdims=True)
+    inverse = lax.rsqrt(jnp.mean(center * center, axis=1, keepdims=True) + NORM_EPS)
+    own = center * inverse * row_of(vec_rows, 0, 16) + row_of(vec_rows, 16, 16)
+    normed[c, x] = own.astype(jnp.bfloat16)
+    forward = gather_tokens(copies, normed)
+    step(forward)
+    dense_here.wait_recv()
+    dense = gather_weights(copies, by_columns(wd, 2048))
+    step(dense)
+    step(into_qkv)
+    qkv = gather_weights(copies, by_rows(wq, 128))
+    step(qkv)
+    for _ in range(4):
+        step(shrink, expand, cotangent, forward, dense, qkv)
+    copies.finish()
+
+
+def gather_all(tokens, d_out, we_send, wq_send, wd_own, ws_own, vec_own):
+    low = jnp.bfloat16
+    vmem = pl.BlockSpec(memory_space=pltpu.VMEM)
+    shapes = [
+        ((4, 4, 128, 1024), low), ((4, 4, 128, 768), low), ((4, 4, 16, 2048), low),
+        ((4, 4, 64, 2048), low), ((2, 4, 128, 2048), low), ((2, 4, 128, 2048), low),
+        ((184, 128), jnp.float32),
+    ]
+    return pl.pallas_call(
+        gather_kernel,
+        in_specs=[vmem] * 7,
+        out_specs=[vmem] * 7,
+        out_shape=[jax.ShapeDtypeStruct(s, t) for s, t in shapes],
+        scratch_shapes=[
+            pltpu.VMEM((4, 4, 2, 4, 8, 128), jnp.float32),
+            pltpu.SemaphoreType.DMA((COPIES,)),
+            pltpu.SemaphoreType.DMA((COPIES,)),
+        ],
+        compiler_params=pltpu.CompilerParams(
+            collective_id=0, has_side_effects=True, vmem_limit_bytes=48 * 2**20
+        ),
+        name="gather_all",
+    )(tokens, d_out, we_send, wq_send, wd_own, ws_own, vec_own)
 
 
 def block_ranks(block_rows):
@@ -199,32 +423,46 @@
     return (second_new, updated)
 
 
-def columns_out(value, chunks):
-    rows = value.shape[0]
-    parts = value.reshape(rows, chunks, TPN, PAIR).transpose(2, 0, 1, 3)
-    parts = parts.reshape(TPN, rows, chunks * PAIR)
-    return lax.all_to_all(parts, TP, split_axis=0, concat_axis=0, tiled=True).reshape(
-        TPN * rows, chunks * PAIR
-    )
-
-
-def columns_back(value, chunks):
-    rows = value.shape[0] // TPN
-    parts = value.reshape(TPN, rows, chunks * PAIR)
-    parts = lax.all_to_all(parts, TP, split_axis=0, concat_axis=0, tiled=True)
-    parts = parts.reshape(TPN, rows, chunks, PAIR).transpose(1, 2, 0, 3)
-    return parts.reshape(rows, chunks * TPN * PAIR)
-
-
-def own_columns(vector, chunks, t):
-    parts = vector.reshape(chunks, TPN, PAIR)
-    return lax.dynamic_index_in_dim(parts, t, axis=1, keepdims=False).reshape(chunks * PAIR)
-
-
-def spread_columns(vector, chunks, t):
-    parts = jnp.zeros((chunks, TPN, PAIR), jnp.float32)
-    parts = lax.dynamic_update_index_in_dim(parts, vector.reshape(chunks, PAIR), t, axis=1)
-    return parts.reshape(-1)
+def qkv_out(value):
+    lead = value.shape[:-1]
+    parts = value.reshape(*lead, 3, 2, TPN, PAIR)[..., ::-1, :, :]
+    return jnp.moveaxis(parts, -2, 0).reshape(TPN, *lead, 6 * PAIR)
+
+
+def qkv_back(parts):
+    lead = parts.shape[1:-1]
+    parts = jnp.moveaxis(parts.reshape(TPN, *lead, 3, 2, PAIR), 0, -2)[..., ::-1, :, :]
+    return parts.reshape(*lead, 3 * MODEL)
+
+
+def expand_out(value):
+    lead = value.shape[:-1]
+    parts = value.reshape(*lead, FF // 512, TPN, 64)
+    return jnp.moveaxis(parts, -2, 0).reshape(TPN, *lead, FF // TPN)
+
+
+def expand_back(parts):
+    lead = parts.shape[1:-1]
+    parts = jnp.moveaxis(parts.reshape(TPN, *lead, FF // 512, 64), 0, -2)
+    return parts.reshape(*lead, FF)
+
+
+def to_group(parts):
+    return lax.all_to_all(parts, TP, split_axis=0, concat_axis=0, tiled=True)
+
+
+def placed(value, t):
+    return lax.dynamic_update_index_in_dim(
+        jnp.zeros((TPN, value.shape[0]), jnp.float32), value, t, axis=0
+    )
+
+
+def dense_route():
+    pairs = []
+    for z, y, c, x in np.ndindex(*SIZES):
+        target = (((1 - z // 2) * 2 + c) * 4 + x) * 8 + (z % 2) * 4 + y
+        pairs.append((((z * 4 + y) * 2 + c) * 4 + x, target))
+    return pairs
 
 
 def gathered(value, axes):
@@ -243,43 +481,47 @@
     shrink_weight, shrink_moment, shrink_second,
     vectors, vec_moment, vec_second,
 ):
-    t = lax.axis_index("c") * 4 + lax.axis_index("x")
+    z, y, c, x = (lax.axis_index(a) for a in ALL)
+    t = c * 4 + x
     low = jnp.bfloat16
-    vec_all = gathered(vectors.astype(low), ALL).astype(jnp.float32)
-    expand_cols = columns_out(expand_weight.astype(low), 8)
-    qkv_cols = columns_out(qkv_weight.astype(low), 6)
-    dense_rows = lax.ppermute(dense_weight.astype(low), ALL, dense_route())
-    shrink_rows = lax.ppermute(shrink_weight.astype(low), ALL, shrink_route())
-    w_expand = gathered(expand_cols, ZY)
-    w_qkv = gathered(qkv_cols, ZY)
-    w_dense = gathered(dense_rows, ZY)
-    w_shrink = gathered(shrink_rows, ZY)
-
-    norm_gain, norm_shift = vec_all[:MODEL], vec_all[MODEL : 2 * MODEL]
-    bias_qkv = own_columns(vec_all[2 * MODEL : 5 * MODEL], 6, t)
-    bias_dense = vec_all[5 * MODEL : 6 * MODEL]
-    bias_expand = own_columns(vec_all[6 * MODEL : 6 * MODEL + FF], 8, t)
-    bias_shrink = vec_all[6 * MODEL + FF :]
-
+    place = lax.rem(((z * 4 + y) * 8 + t) * 176, 128)
+    vec_own = lax.dynamic_update_slice(
+        jnp.zeros((1024,), jnp.float32), vectors.astype(low).astype(jnp.float32), (place,)
+    ).reshape(8, 128)
     block_rows = gathered(block_seq, "c")
     length_rows = gathered(seq_lengths, "c")
     ranks = block_ranks(block_rows)
     limits = jnp.where(block_rows == 0, length_rows[:, :1], length_rows[:, 1:])
 
-    c, x = lax.axis_index("c"), lax.axis_index("x")
     my_rank = lax.dynamic_index_in_dim(ranks[c], x, keepdims=False)
     my_limit = lax.dynamic_index_in_dim(limits[c], x, keepdims=False)
     live = my_rank * BLOCK + jnp.arange(BLOCK, dtype=jnp.int32) < my_limit
+
+    d_out_own = jnp.where(live[:, None], cotangent, jnp.zeros_like(cotangent))
+    w_expand, w_qkv, w_dense, w_shrink, normed, d_out, vec_rows = gather_all(
+        tokens,
+        d_out_own,
+        expand_out(expand_weight.astype(low)),
+        qkv_out(qkv_weight.astype(low)),
+        dense_weight.astype(low),
+        shrink_weight.astype(low),
+        vec_own,
+    )
+    w_expand, w_qkv = w_expand.reshape(MODEL, -1), w_qkv.reshape(MODEL, -1)
+    w_dense, w_shrink = w_dense.reshape(-1, MODEL), w_shrink.reshape(-1, MODEL)
+    normed, d_out = normed.reshape(-1, MODEL), d_out.reshape(-1, MODEL)
+    vec_all = vec_rows[:176].reshape(-1)
+    norm_gain = vec_all[:MODEL]
+    bias_qkv = qkv_out(vec_all[2 * MODEL : 5 * MODEL])[t]
+    bias_dense = vec_all[5 * MODEL : 6 * MODEL]
+    bias_expand = expand_out(vec_all[6 * MODEL : 6 * MODEL + FF])[t]
+    bias_shrink = vec_all[6 * MODEL + FF :]
 
     inputs = tokens.astype(jnp.float32)
     mean = jnp.mean(inputs, axis=1, keepdims=True)
     center = inputs - mean
     inverse = lax.rsqrt(jnp.mean(center * center, axis=1, keepdims=True) + NORM_EPS)
     xhat = center * inverse
-    normed_own = (xhat * norm_gain + norm_shift).astype(low)
-    d_out_own = jnp.where(live[:, None], cotangent, jnp.zeros_like(cotangent))
-    normed = gathered(normed_own, TP)
-    d_out = gathered(d_out_own, TP)
 
     pre = dot(normed, w_expand) + bias_expand
     inner = jnp.tanh(GELU_A * (pre + GELU_B * (pre * pre * pre)))
@@ -322,18 +564,18 @@
         [
             jnp.sum(d_normed * xhat, axis=0),
             jnp.sum(d_normed, axis=0),
-            spread_columns(jnp.sum(d_qkv, axis=0, dtype=jnp.float32), 6, t),
+            qkv_back(placed(jnp.sum(d_qkv, axis=0, dtype=jnp.float32), t)),
             d_out_sum,
-            spread_columns(jnp.sum(d_pre, axis=0, dtype=jnp.float32), 8, t),
+            expand_back(placed(jnp.sum(d_pre, axis=0, dtype=jnp.float32), t)),
             d_out_sum,
         ]
     )
     vec_grad = summed(vec_terms, ALL)
 
-    shrink_grad = lax.ppermute(shrink_sum, ALL, back(shrink_route())).astype(jnp.float32)
-    dense_grad = lax.ppermute(dense_sum, ALL, back(dense_route())).astype(jnp.float32)
-    qkv_grad = columns_back(qkv_sum, 6).astype(jnp.float32)
-    expand_grad = columns_back(expand_sum, 8).astype(jnp.float32)
+    shrink_grad = shrink_sum.astype(jnp.float32)
+    dense_grad = lax.ppermute(dense_sum, ALL, dense_route()).astype(jnp.float32)
+    qkv_grad = qkv_back(to_group(qkv_sum.reshape(TPN, 16, -1))).astype(jnp.float32)
+    expand_grad = expand_back(to_group(expand_sum.reshape(TPN, 16, -1))).astype(jnp.float32)
 
     masters = (qkv_weight, dense_weight, expand_weight, shrink_weight, vectors)
     moments = (qkv_moment, dense_moment, expand_moment, shrink_moment, vec_moment)

time: 945 us -> 736 us (0.78)
  waiting for transfers between devices: 655 us -> 465 us
  Pallas kernels: 18.5 us -> 119 us
  blocking collectives: 94.1 us -> 5.04 us
  starting transfers between devices: 33.2 us -> 18.3 us
  matrix products: 82 us -> 72.5 us
    all_gather x6 -> x0, waiting for transfers between devices: 169 us -> none  [gathered(): return lax.all_gather(value, axes, axis=0, tiled=True)]
    pallas_call x0 -> x1, Pallas kernels: none -> 101 us  [gather_all(): pl.pallas_call(gather_kernel, in_specs=[vmem] * 7, out_specs=[vmem] * 7,...]
    unnamed x1 -> x0, blocking collectives: 69.3 us -> none
    all_to_all x2 -> x0, blocking collectives: 21.3 us -> none  [columns_out(): lax.all_to_all(parts, TP, split_axis=0, concat_axis=0, tiled=True)]
    ppermute x4 -> x1, starting transfers between devices: 19 us -> 4.24 us  [shards(): dense_grad = lax.ppermute(dense_sum, ALL, dense_route()).astype(jnp.float32)]
    ppermute x4 -> x1, waiting for transfers between devices: 14.3 us -> 0.01 us  [shards(): dense_grad = lax.ppermute(dense_sum, ALL, dense_route()).astype(jnp.float32)]
    unnamed x14 -> x8, waiting for transfers between devices: 141 us -> 141 us
  transfers between devices with their start and end apart: 19 -> 10, of which waited for: 17 -> 8; matrix products, arithmetic and copies ran while one was open for 10% -> 11% of each run, Pallas kernels for 2% -> 0%
where the time goes in v2:
time: 736 us; the launch traced here: 733 us
  waiting for transfers between devices  465 us (63%)
  Pallas kernels  119 us (16%)
  matrix products  72.5 us (10%)
  other arithmetic  20.3 us (3%)
  starting transfers between devices  18.3 us (2%)
  local copies, waits for them, and re-layouts  16.5 us (2%)
  between operations  15.8 us (2%)
    reduce_scatter x6, waiting for transfers between devices, summed(): return lax.psum_scatter(value, axes, scatter_dimension=0, tiled=True)  319 us
    unnamed x8, waiting for transfers between devices  141 us
    pallas_call x1, Pallas kernels, gather_all(): pl.pallas_call(gather_kernel, in_specs=[vmem] * 7, out_specs=[vmem] * 7,...  101 us
    dot_general x4, matrix products, cross(): lax.dot_general(a, b, (((0,), (0,)), ((), ())), preferred_element_type=jn...  26.5 us
    dot_general x4, matrix products, dot(): return jnp.dot(a, b, preferred_element_type=jnp.float32)  25.6 us
    dot_general x4, matrix products, dot_t(): lax.dot_general(a, b, (((1,), (1,)), ((), ())), preferred_element_type=jn...  20.4 us
    pallas_call x1, Pallas kernels, attention(): pl.pallas_call(attention_kernel, grid=(rows // GROUP, 2), in_specs=[smem,...  18.4 us
  transfers between devices with their start and end apart: 10, of which 8 were waited for; matrix products, arithmetic and copies ran while one was open for 11% of the time, Pallas kernels for 0%

profile of v2, /device:TPU:1, one launch (start us, length us, event | category | flops | bytes accessed | tf_op | source)
XLA Modules:
  0.0 732.7 jit_solution(2047241720101042650)
XLA Ops:
  7.3 3.2 all-gather
  21.6 100.8 %gather_all.1 = (bf16[4,4,128,1024]{3,2,1,0:T(8,128)(2,1)}, bf16[4,4,128,768]{3,2,1,0:T(8,128)(2,1)S(1)}, bf16[4,4,16,2048]{3,2,1,0:T(8,128)(2,1)S(1)}, bf16[4,4...) custom-call(bf16[128,2048]{1,0:T(8,128)(2,1)S(1)} %copy-done, ...), custom_call_target="tpu_custom_call" | custom-call | tf_op jit(solution)/shard_map/gather_all/pallas_call | solution.py:295
  124.0 6.1 convolution_add_fusion
  133.8 18.4 %attention.1 = (bf16[1024,256]{1,0:T(8,128)(2,1)S(1)}, bf16[1024,256]{1,0:T(8,128)(2,1)S(1)}, bf16[1024,256]{1,0:T(8,128)(2,1)S(1)}, bf16[1024,256]{1,0:T(8,128)(2,1)S(1)}) custom-call(s32[2,4]{1,0:T(2,128)S(1)} %bitcast.83, s32[2,4]{1,0:T(2,128)S(1)} %select_reduce_fusion.rank_ref, s32[2,4]{1,0:T(2,128)S(1)} %compare_select_fusion.limit_ref, ...), custom_call_target="tpu_custom_call" | custom-call | flops 2000000000 | bytes 6291456 | tf_op jit(solution)/shard_map/attention/pallas_call | solution.py:395
  159.6 7.4 %convolution_convert_fusion.2 = bf16[2048,768]{1,0:T(8,128)(2,1)} fusion(bf16[1024,2048]{1,0:T(8,128)(2,1)} %bitcast.114, bf16[1024,768]{1,0:T(8,128)(2,1)S(1)} %constant_dynamic-update-slice_fusion), kind=kOutput, calls=%fused_computation.18 | convolution fusion | flops 3222798336 | bytes 8912896 | tf_op jit(solution)/shard_map/dot_general | solution.py:49
  167.4 7.7 %fusion.35 = f32[1024,1024]{1,0:T(8,128)S(1)} fusion(bf16[1024,2048]{1,0:T(8,128)(2,1)} %bitcast.115, bf16[2048,1024]{1,0:T(8,128)(2,1)} %bitcast.111), kind=kOutput, calls=%fused_computation.94 | convolution fusion | flops 4294967296 | bytes 12582912 | tf_op jit(solution)/shard_map/dot_general | solution.py:41
  175.1 6.9 convert_reduce_fusion
  183.5 6.2 convolution_convert_fusion.1
  190.0 6.0 fusion.36
  196.0 6.1 add_convert_fusion
  202.2 10.6 %convolution_convert_fusion = bf16[1024,2048]{1,0:T(8,128)(2,1)} fusion(bf16[1024,2048]{1,0:T(8,128)(2,1)} %bitcast.107, f32[1024,1024]{1,0:T(8,128)} %copy-done.29, f32[1024]{0:T(1024)S(1)} %bitcast.103), kind=kOutput, calls=%fused_computation.16 | convolution fusion | flops 4307550208 | bytes 12587008 | tf_op jit(solution)/shard_map/dot_general | solution.py:49
  213.2 8.4 %fusion.28 = f32[1024,2048]{1,0:T(8,128)S(1)} fusion(bf16[1024,2048]{1,0:T(8,128)(2,1)} %bitcast.105, f32[1024,1024]{1,0:T(8,128)} %copy-done.29, f32[1024]{0:T(1024)S(1)} %bitcast.104), kind=kOutput, calls=%fused_computation.92 | convolution fusion | flops 4305453056 | bytes 16781312 | tf_op jit(solution)/shard_map/dot_general | solution.py:41
  221.5 3.4 add_convert_fusion.1
  226.9 4.2 collective-permute-start
  231.9 73.8 %reduce-scatter.11.cloned.1.call-done = bf16[128,768]{1,0:T(8,128)(2,1)} async-done(((bf16[2048,768]{1,0:T(8,128)(2,1)}), bf16[128,768]{1,0:T(8,128)(2,1)}) %reduce-scatter.11.cloned.1.call-update) | async-done | bytes 196624 | tf_op jit(solution)/shard_map/reduce_scatter | solution.py:473
  305.7 6.6 all-to-all-start
  313.9 4.2 all-to-all-done
  320.6 65.7 %reduce-scatter.15.cloned.1.call-done = bf16[128,1024]{1,0:T(8,128)(2,1)} async-done(((bf16[2048,1024]{1,0:T(8,128)(2,1)}), bf16[128,1024]{1,0:T(8,128)(2,1)}) %reduce-scatter.15.cloned.1.call-update) | async-done | bytes 262160 | tf_op jit(solution)/shard_map/reduce_scatter | solution.py:473
  386.3 6.7 all-to-all-start.1
  393.0 48.7 %reduce-scatter.9.cloned.1.call-done = bf16[128,2048]{1,0:T(8,128)(2,1)} async-done(((bf16[1024,2048]{1,0:T(8,128)(2,1)}), bf16[128,2048]{1,0:T(8,128)(2,1)}) %reduce-scatter.9.cloned.1.call-update) | async-done | bytes 524304 | tf_op jit(solution)/shard_map/reduce_scatter | solution.py:473
  444.0 76.8 %reduce-scatter.17.cloned.1.call-done = bf16[64,2048]{1,0:T(8,128)(2,1)} async-done(((bf16[1024,2048]{1,0:T(8,128)(2,1)}), bf16[64,2048]{1,0:T(8,128)(2,1)}) %reduce-scatter.17.cloned.1.call-update) | async-done | bytes 262160 | tf_op jit(solution)/shard_map/reduce_scatter | solution.py:473
  523.4 52.9 %reduce-scatter.7.cloned.1.call-done = bf16[128,2048]{1,0:T(8,128)(2,1)} async-done(((bf16[1024,2048]{1,0:T(8,128)(2,1)}), bf16[128,2048]{1,0:T(8,128)(2,1)}) %reduce-scatter.7.cloned.1.call-update) | async-done | bytes 524304 | tf_op jit(solution)/shard_map/reduce_scatter | solution.py:473
  576.3 2.7 fusion.19
  578.9 141.4 %all-reduce.3.cloned.1.call-done = f32[22528]{0:T(1024)} async-done(((f32[22528]{0:T(1024)}), f32[22528]{0:T(1024)}) %all-reduce.3.cloned.1.call-update) | async-done | bytes 90128
  (152 shorter events, 42.1 us)
Async XLA Ops:
  7.2 12.1 %copy-start.10 = (f32[64,2048]{1,0:T(8,128)S(1)}, f32[64,2048]{1,0:T(8,128)}, u32[]{:S(2)}) copy-start(f32[64,2048]{1,0:T(8,128)} %param.35) | copy-start | bytes 1572868
  7.2 13.5 %copy-start.15 = (bf16[128,2048]{1,0:T(8,128)(2,1)S(1)}, bf16[128,2048]{1,0:T(8,128)(2,1)}, u32[]{:S(2)}) copy-start(bf16[128,2048]{1,0:T(8,128)(2,1)} %param.23) | copy-start | bytes 1572868
  7.2 13.7 %copy-start.21 = (f32[176]{0:T(256)S(1)}, f32[176]{0:T(256)}, u32[]{:S(2)}) copy-start(f32[176]{0:T(256)} %param.38) | copy-start | bytes 2116
  7.2 14.3 %copy-start = (bf16[128,2048]{1,0:T(8,128)(2,1)S(1)}, bf16[128,2048]{1,0:T(8,128)(2,1)}, u32[]{:S(2)}) copy-start(bf16[128,2048]{1,0:T(8,128)(2,1)} %tokens_ref.1) | copy-start | bytes 1572868
  7.2 219.7 %reduce-scatter.13.cloned.1.call-start = ((), (), s32[]{:S(2)}) async-start(), calls=%async_computation.11 | async-start | bytes 1114112 | tf_op jit(solution)/shard_map/reduce_scatter | solution.py:473
  156.1 149.6 %reduce-scatter.11.cloned.1.call-start = ((), (), s32[]{:S(2)}) async-start(), calls=%async_computation.10 | async-start | bytes 3342336 | tf_op jit(solution)/shard_map/reduce_scatter | solution.py:473
  167.1 219.3 %reduce-scatter.15.cloned.1.call-start = ((), (), s32[]{:S(2)}) async-start(), calls=%async_computation.12 | async-start | bytes 4456448 | tf_op jit(solution)/shard_map/reduce_scatter | solution.py:473
  189.7 252.0 %reduce-scatter.9.cloned.1.call-start = ((), (), s32[]{:S(2)}) async-start(), calls=%async_computation.9 | async-start | bytes 4718592 | tf_op jit(solution)/shard_map/reduce_scatter | solution.py:473
  202.1 318.7 %reduce-scatter.17.cloned.1.call-start = ((), (), s32[]{:S(2)}) async-start(), calls=%async_computation.13 | async-start | bytes 4456448 | tf_op jit(solution)/shard_map/reduce_scatter | solution.py:473
  212.9 363.4 %reduce-scatter.7.cloned.1.call-start = ((), (), s32[]{:S(2)}) async-start(), calls=%async_computation.8 | async-start | bytes 4718592 | tf_op jit(solution)/shard_map/reduce_scatter | solution.py:473
  224.9 87.4 %copy-start.16 = (f32[16,2048]{1,0:T(8,128)S(1)}, f32[16,2048]{1,0:T(8,128)}, u32[]{:S(2)}) copy-start(f32[16,2048]{1,0:T(8,128)} %param.29) | copy-start | bytes 393220
  224.9 87.4 %copy-start.18 = (f32[16,2048]{1,0:T(8,128)S(1)}, f32[16,2048]{1,0:T(8,128)}, u32[]{:S(2)}) copy-start(f32[16,2048]{1,0:T(8,128)} %param.30) | copy-start | bytes 393220
  224.9 87.4 %copy-start.19 = (f32[16,2048]{1,0:T(8,128)S(1)}, f32[16,2048]{1,0:T(8,128)}, u32[]{:S(2)}) copy-start(f32[16,2048]{1,0:T(8,128)} %param.31) | copy-start | bytes 393220
  224.9 93.4 %copy-start.14 = (f32[16,6144]{1,0:T(8,128)S(1)}, f32[16,6144]{1,0:T(8,128)}, u32[]{:S(2)}) copy-start(f32[16,6144]{1,0:T(8,128)} %param.26) | copy-start | bytes 1179652
  226.9 85.4 %collective-permute-start = (bf16[16,2048]{1,0:T(8,128)(2,1)}, bf16[16,2048]{1,0:T(8,128)(2,1)}, u32[]{:S(2)}, u32[]{:S(2)}) collective-permute-start(bf16[16,2048]{1,0:T(8,128)(2,1)} %reduce-scatter.13.cloned.1.call-done), channel_id=1, source_target_pairs={{0,64},{1,72},{2,80},{3,88},{4,96},{5,104},{6,112},{7,120},{8,65},... | collective-permute-start | bytes 196616 | tf_op jit(solution)/shard_map/ppermute | solution.py:576
  231.4 289.4 %copy-start.11 = (f32[64,2048]{1,0:T(8,128)S(1)}, f32[64,2048]{1,0:T(8,128)}, u32[]{:S(2)}) copy-start(f32[64,2048]{1,0:T(8,128)} %param.35) | copy-start | bytes 1572868
  305.7 12.4 %all-to-all-start = ((bf16[8,16,768]{2,1,0:T(8,128)(2,1)}), bf16[8,16,768]{2,1,0:T(8,128)(2,1)S(1)}, u32[]{:S(2)}, u32[]{:S(2)}) async-start(bf16[8,16,768]{2,1,0:T(8,128)(2,1)} %bitcast.95), calls=%async_computation.3 | async-start | bytes 393216 | tf_op jit(solution)/shard_map/all_to_all | solution.py:451
  386.3 334.0 %copy-start.22 = (f32[176]{0:T(256)S(1)}, f32[176]{0:T(256)}, u32[]{:S(2)}) copy-start(f32[176]{0:T(256)} %param.39) | copy-start | bytes 2116
  386.3 334.0 %copy-start.23 = (f32[176]{0:T(256)S(1)}, f32[176]{0:T(256)}, u32[]{:S(2)}) copy-start(f32[176]{0:T(256)} %param.40) | copy-start | bytes 2116
  386.3 335.3 %all-to-all-start.1 = ((bf16[8,16,1024]{2,1,0:T(8,128)(2,1)}), bf16[8,16,1024]{2,1,0:T(8,128)(2,1)S(1)}, u32[]{:S(2)}, u32[]{:S(2)}) async-start(bf16[8,16,1024]{2,1,0:T(8,128)(2,1)} %bitcast.92), calls=%async_computation.6 | async-start | bytes 524288 | tf_op jit(solution)/shard_map/all_to_all | solution.py:451
  393.0 327.3 %all-reduce.3.cloned.1.call-start = ((), (), s32[]{:S(2)}) async-start(), calls=%async_computation.14 | async-start | bytes 180224
  441.7 134.6 %copy-start.13 = (bf16[128,2048]{1,0:T(8,128)(2,1)S(1)}, bf16[128,2048]{1,0:T(8,128)(2,1)}, u32[]{:S(2)}) copy-start(bf16[128,2048]{1,0:T(8,128)(2,1)} %reduce-scatter.9.cloned.1.call-done) | copy-start | bytes 1572868
  523.4 199.6 %copy-start.12 = (f32[16,8192]{1,0:T(8,128)S(1)}, f32[16,8192]{1,0:T(8,128)}, u32[]{:S(2)}) copy-start(f32[16,8192]{1,0:T(8,128)} %param.32) | copy-start | bytes 1572868
  523.4 199.6 %copy-start.17 = (f32[16,8192]{1,0:T(8,128)S(1)}, f32[16,8192]{1,0:T(8,128)}, u32[]{:S(2)}) copy-start(f32[16,8192]{1,0:T(8,128)} %param.33) | copy-start | bytes 1572868
  (18 other events, 64.4 us)
Sparse Core Ops, SparseCore 0:
  156.2 70.6 reduce-scatter.12
  230.6 75.0 reduce-scatter.10
  309.4 76.8 reduce-scatter.14
  388.6 53.0 reduce-scatter.8
  444.9 75.9 reduce-scatter.16
  523.2 52.9 reduce-scatter.6
  582.3 137.9 all-reduce.2

commit v3 on v2

v3 whole, which is shorter than its diff:
```python
import functools

import jax
import jax.numpy as jnp
import numpy as np
from jax import lax
from jax.experimental import pallas as pl
from jax.experimental.pallas import tpu as pltpu
from jax.sharding import Mesh
from jax.sharding import PartitionSpec as P

HEAD = 64
ROT = 32
BLOCK = 128
STEP = 10
GROUP = 512
MODEL = 2048
FF = 8192
PAIR = 2 * HEAD
ALL = ("z", "y", "c", "x")
DP = ("z", "y", "c")
ZY = ("z", "y")
TP = ("c", "x")
SIZES = (4, 4, 2, 4)
TPN = 8
COPIES = 320
SCALE = HEAD ** (-0.5)

NORM_EPS = 1e-05
MASKED = -1e30
BETA_ONE = 0.9
BETA_TWO = 0.999
ADAM_EPS = 1e-08
RATES = (0.02, 0.1, 0.02, 0.01, 0.4)
DECAYS = (0.1, 0.1, 0.1, 0.1, 0.0)
GELU_A = float(np.sqrt(2.0 / np.pi))
GELU_B = 0.044715


def dot(a, b):
    return jnp.dot(a, b, preferred_element_type=jnp.float32)


def dot_t(a, b):
    return lax.dot_general(a, b, (((1,), (1,)), ((), ())), preferred_element_type=jnp.float32)


def cross(a, b):
    return lax.dot_general(a, b, (((0,), (0,)), ((), ())), preferred_element_type=jnp.float32)


def rotary_constants():
    half = np.arange(ROT // 2, dtype=np.float32)
    inverse = (10000.0 ** (-2.0 * half.astype(np.float64) / ROT)).astype(np.float32)
    angle = (np.arange(GROUP, dtype=np.float32)[:, None] * inverse[None, :]).astype(np.float64)
    cosine, sine = np.cos(angle).astype(np.float32), np.sin(angle).astype(np.float32)
    one = np.ones((GROUP, HEAD - ROT), np.float32)
    zero = np.zeros((GROUP, ROT // 2), np.float32)
    rest = np.zeros((GROUP, HEAD - ROT), np.float32)
    turn = np.concatenate([cosine, cosine, one], axis=1)
    ahead = np.concatenate([-sine, zero, rest], axis=1)
    behind = np.concatenate([zero, sine, rest], axis=1)
    return tuple(np.concatenate([a, a], axis=1) for a in (turn, ahead, behind))


MESH = pl.DeviceIdType.MESH


def other(axis, step):
    size = SIZES[ALL.index(axis)]
    return lax.rem(lax.axis_index(axis) + step + size, size)


class Copies:
    def __init__(self, send, recv):
        self.send, self.recv, self.count, self.open = send, recv, 0, []

    def start(self, src, dst, to):
        at = self.count
        self.count += 1
        copy = pltpu.make_async_remote_copy(
            src_ref=src,
            dst_ref=dst,
            send_sem=self.send.at[at],
            recv_sem=self.recv.at[at],
            device_id=to,
            device_id_type=MESH,
        )
        copy.start()
        self.open.append(copy)
        return copy

    def sent(self, *copies):
        for copy in copies:
            copy.wait_send()
            self.open = [each for each in self.open if each is not copy]

    def finish(self):
        self.sent(*list(self.open))


def enter():
    barrier = pltpu.get_barrier_semaphore()
    for partner in token_partners() + weight_partners() + [dense_partner()]:
        pl.semaphore_signal(barrier, inc=1, device_id=partner, device_id_type=MESH)
    pl.semaphore_wait(barrier, 23)


def token_partners():
    return [{"c": other("c", i), "x": other("x", j)} for i in range(2) for j in range(4) if i + j]


def weight_partners():
    return [{"z": other("z", i), "y": other("y", j)} for i in range(4) for j in range(4) if i + j]


def dense_partner():
    z, y, c, x = (lax.axis_index(a) for a in ALL)
    return {"z": (1 - z // 2) * 2 + c, "y": x, "c": lax.rem(z, 2), "x": y}


def gather_weights(copies, view):
    z, y = lax.axis_index("z"), lax.axis_index("y")
    up, down = {"y": other("y", 1)}, {"y": other("y", -1)}
    far, near = {"z": other("z", 1)}, {"z": other("z", -1)}
    every = slice(None)

    def go(block, to):
        return copies.start(block, block, to)

    a_up, a_down = go(view(z, y, 4), up), go(view(z, y, 4), down)
    b_far, b_near = go(view(z, y, 5), far), go(view(z, y, 5), near)
    yield
    a_up.wait_recv()
    a_up = go(view(z, other("y", -1), 0), up)
    b_far.wait_recv()
    b_far = go(view(other("z", -1), y, 2), far)
    a_down.wait_recv()
    a_down = go(view(z, other("y", 1), 1), down)
    b_near.wait_recv()
    b_near = go(view(other("z", 1), y, 3), near)
    yield
    a_up.wait_recv()
    a_down.wait_recv()
    a_far, a_near = go(view(z, every, 4), far), go(view(z, every, 4), near)
    b_far.wait_recv()
    b_near.wait_recv()
    b_up, b_down = go(view(every, y, 5), up), go(view(every, y, 5), down)
    yield
    a_far.wait_recv()
    a_far = go(view(other("z", -1), every, 0), far)
    b_up.wait_recv()
    b_up = go(view(every, other("y", -1), 2), up)
    a_near.wait_recv()
    a_near = go(view(other("z", 1), every, 1), near)
    b_down.wait_recv()
    b_down = go(view(every, other("y", 1), 3), down)
    yield
    for copy in (a_far, a_near, b_up, b_down):
        copy.wait_recv()


def gather_tokens(copies, ref):
    c, x, across = lax.axis_index("c"), lax.axis_index("x"), other("c", 1)
    mine = []

    def go(block, to):
        mine.append(copies.start(block, block, to))
        return mine[-1]

    own = ref.at[c, x]
    right, left, core = go(own, {"x": other("x", 1)}), go(own, {"x": other("x", -1)}), [go(own, {"c": across})]
    yield
    right.wait_recv()
    came = ref.at[c, other("x", -1)]
    right = go(ref.at[c, other("x", -1), pl.ds(0, 64)], {"x": other("x", 1)})
    core.append(go(came, {"c": across}))
    left.wait_recv()
    came = ref.at[c, other("x", 1)]
    left = go(ref.at[c, other("x", 1), pl.ds(64, 64)], {"x": other("x", -1)})
    core.append(go(came, {"c": across}))
    yield
    right.wait_recv()
    left.wait_recv()
    core.append(go(ref.at[c, other("x", 2)], {"c": across}))
    yield
    for copy in core:
        copy.wait_recv()
    copies.sent(*mine)


def gather_vectors(copies, ref):
    z, y, c, x = (lax.axis_index(a) for a in ALL)
    sent = [copies.start(ref.at[z, y, c, x], ref.at[z, y, c, x], to) for to in token_partners()]
    yield
    for copy in sent:
        copy.wait_recv()
    sent = [copies.start(ref.at[z, y], ref.at[z, y], to) for to in weight_partners()]
    yield
    for copy in sent:
        copy.wait_recv()


def expand_to_group(copies, send, ref, width):
    z, y, c, x = (lax.axis_index(a) for a in ALL)
    rows = pl.ds(pl.multiple_of((c * 4 + x) * 16, 16), 16)
    sent = []
    for to in token_partners():
        sent.append(copies.start(send.at[to["c"] * 4 + to["x"]], ref.at[z, y, rows], to))
    ref[z, y, rows] = send[c * 4 + x]
    yield
    for copy in sent:
        copy.wait_recv()


def by_rows(ref, rows):
    quarter = rows // 4

    def view(z, y, part):
        start, size = (part * quarter, quarter) if part < 4 else ((part - 4) * 2 * quarter, 2 * quarter)
        return ref.at[z, y, pl.ds(start, size)]

    return view


def by_columns(ref, columns):
    quarter = columns // 4

    def view(z, y, part):
        start, size = (part * quarter, quarter) if part < 4 else ((part - 4) * 2 * quarter, 2 * quarter)
        return ref.at[z, y, :, pl.ds(start, size)]

    return view


def step(*works):
    for work in works:
        next(work, None)


def row_of(ref, first, count):
    return jnp.concatenate([ref[pl.ds(first + i, 1), :] for i in range(count)], axis=1)


def ring_sum(copies, axis, block, land, low_part, high_part):
    ahead, behind = other(axis, 1), other(axis, -1)
    up, down = {axis: ahead}, {axis: behind}
    far = other(axis, 2)
    t_low = copies.start(block(far, low_part), land.at[0], up)
    t_high = copies.start(block(far, high_part), land.at[1], down)
    d_high = copies.start(block(ahead, high_part), land.at[3], up)
    d_low = copies.start(block(behind, low_part), land.at[2], down)
    yield
    t_low.wait_recv()
    land[0] = land[0] + block(ahead, low_part)[...]
    p_low = copies.start(land.at[0], land.at[4], up)
    t_high.wait_recv()
    land[1] = land[1] + block(behind, high_part)[...]
    p_high = copies.start(land.at[1], land.at[5], down)
    yield
    for copy in (d_low, d_high, p_low, p_high):
        copy.wait_recv()
    copies.sent(t_low, t_high, d_low, d_high, p_low, p_high)


def three(own, land, high, at=...):
    f32 = jnp.float32
    first, second = land.at[4 + high], land.at[2 + high]
    return own[at].astype(f32) + first[at].astype(f32) + second[at].astype(f32)


def both(first, second):
    while True:
        done = [next(first, 0), next(second, 0)]
        if 0 in done:
            return
        yield


def scatter_weights(copies, view, wide, narrow, give):
    z, y = lax.axis_index("z"), lax.axis_index("y")
    every = slice(None)
    low = jnp.bfloat16
    yield from both(
        ring_sum(copies, "y", lambda i, p: view(every, i, p), wide.at[0], 0, 1),
        ring_sum(copies, "z", lambda i, p: view(i, every, p), wide.at[1], 2, 3),
    )
    for high in range(2):
        own = view(every, y, high)
        for i in range(4):
            own[i] = three(own, wide.at[0], high, i).astype(low)
        own = view(z, every, 2 + high)
        for i in range(4):
            own[i] = three(own, wide.at[1], high, i).astype(low)
    yield from both(
        ring_sum(copies, "z", lambda i, p: view(i, y, p), narrow.at[0], 0, 1),
        ring_sum(copies, "y", lambda i, p: view(z, i, p), narrow.at[1], 2, 3),
    )
    for high in range(2):
        give(high, three(view(z, y, high), narrow.at[0], high))
        give(2 + high, three(view(z, y, 2 + high), narrow.at[1], high))


def scatter_tokens(copies, ref, core_land, land, give, core_free, ring_free, first):
    c, x, across = lax.axis_index("c"), lax.axis_index("x"), other("c", 1)
    if not first:
        pl.semaphore_wait(core_free, 1)
    came = copies.start(ref.at[across], core_land, {"c": across})
    yield
    came.wait_recv()
    for i in range(4):
        ref[c, i] = ref[c, i] + core_land[i]
    if first:
        pl.semaphore_signal(core_free, inc=1, device_id={"c": across}, device_id_type=MESH)
    else:
        pl.semaphore_wait(ring_free, 2)
    yield from ring_sum(copies, "x", lambda i, p: ref.at[c, i, pl.ds(p * 64, 64)], land, 0, 1)
    for high in range(2):
        own = ref.at[c, x, pl.ds(high * 64, 64)]

        def chunk(r, _):
            rows = pl.ds(pl.multiple_of(r * 16, 16), 16)
            give(pl.ds(pl.multiple_of(high * 64 + r * 16, 16), 16), three(own, land, high, rows))
            return 0

        lax.fori_loop(0, 4, chunk, 0)
    if first:
        for way in (1, -1):
            to = {"x": other("x", way)}
            pl.semaphore_signal(ring_free, inc=1, device_id=to, device_id_type=MESH)


def return_to_group(copies, ref, out):
    c, x = lax.axis_index("c"), lax.axis_index("x")
    t = c * 4 + x
    sent = []
    for to in token_partners():
        sent.append(copies.start(ref.at[to["c"] * 4 + to["x"]], out.at[t], to))
    out[t] = ref[t]
    yield
    for copy in sent:
        copy.wait_recv()


def turned(values, table, sign):
    turn, ahead, behind = table
    up = pltpu.roll(values, PAIR - ROT // 2, 1)
    down = pltpu.roll(values, ROT // 2, 1)
    if sign > 0:
        return values * turn + up * ahead + down * behind
    return values * turn - up * ahead - down * behind


def attend(meta, turn_ref, qkv, att, g, p):
    low, f32 = jnp.bfloat16, jnp.float32
    lane = lax.broadcasted_iota(jnp.int32, (BLOCK, PAIR), 1)
    first = lane < HEAD
    zero = jnp.zeros((BLOCK, PAIR), low)
    row_at = lax.broadcasted_iota(jnp.int32, (BLOCK, BLOCK), 0)
    col_at = lax.broadcasted_iota(jnp.int32, (BLOCK, BLOCK), 1)
    cols = [pl.ds(pl.multiple_of(i * 2 * PAIR + p * PAIR, PAIR), PAIR) for i in range(3)]
    d_k = [jnp.zeros((BLOCK, PAIR), f32) for _ in range(4)]
    d_v = [jnp.zeros((BLOCK, PAIR), f32) for _ in range(4)]
    for b in range(4):
        rows, width = pl.ds(b * BLOCK, BLOCK), (b + 1) * BLOCK
        keys = pl.ds(0, width)
        base = meta[:, 4 + b : 5 + b] * BLOCK
        diagonal = (col_at <= row_at) & (col_at.astype(f32) + base < meta[:, 8 + b : 9 + b])
        bias = [
            jnp.where(meta[:, e : e + 1] == meta[:, b : b + 1], 0.0, MASKED)
            + jnp.zeros((BLOCK, BLOCK), f32)
            for e in range(b)
        ]
        bias.append(jnp.where(diagonal, 0.0, MASKED).astype(f32))
        bias = bias[0] if b == 0 else jnp.concatenate(bias, axis=1)
        q, da = qkv[g, rows, cols[0]], att[g, rows, cols[0]]
        k, v = qkv[g, keys, cols[1]], qkv[g, keys, cols[2]]
        qs = [jnp.where(first, q, zero), jnp.where(first, zero, q)]
        das = [jnp.where(first, da, zero), jnp.where(first, zero, da)]
        atts, probs, dss = [], [], []
        for h in range(2):
            s = dot_t(qs[h], k) + bias
            w = jnp.exp(s - jnp.max(s, axis=1, keepdims=True))
            prob = w * (1.0 / jnp.sum(w, axis=1, keepdims=True))
            probs.append(prob.astype(low))
            atts.append(dot(probs[h], v))
            dp = dot_t(das[h], v)
            dss.append((prob * (dp - jnp.sum(prob * dp, axis=1, keepdims=True))).astype(low))
        att[g, rows, cols[0]] = jnp.where(first, atts[0], atts[1]).astype(low)
        dq = jnp.where(first, dot(dss[0], k), dot(dss[1], k)) * SCALE
        qkv[g, rows, cols[0]] = turned(dq, table_of(meta, turn_ref, b), -1).astype(low)
        dk = cross(jnp.concatenate(dss, axis=0), jnp.concatenate(qs, axis=0))
        dv = cross(jnp.concatenate(probs, axis=0), jnp.concatenate(das, axis=0))
        for e in range(b + 1):
            d_k[e] = d_k[e] + dk[e * BLOCK : (e + 1) * BLOCK]
            d_v[e] = d_v[e] + dv[e * BLOCK : (e + 1) * BLOCK]
    for b in range(4):
        rows = pl.ds(b * BLOCK, BLOCK)
        qkv[g, rows, cols[1]] = turned(d_k[b], table_of(meta, turn_ref, b), -1).astype(low)
        qkv[g, rows, cols[2]] = d_v[b].astype(low)


def table_of(meta, turn_ref, b):
    rank = meta[:, 4 + b : 5 + b]
    parts = [turn_ref[:, pl.ds(r * BLOCK, BLOCK), :] for r in range(3)]
    table = jnp.where((rank == 0.0)[None], parts[0], jnp.where((rank == 1.0)[None], parts[1], parts[2]))
    return table[0], table[1], table[2]


def layer_kernel(
    tokens_ref, cot_ref, we_send, wq_send, wd_own, ws_own, vec_own, turn_ref,
    out_ref, ig_ref, ge_out, gq_out, gd_out, gs_out, vec_out,
    we, wq, wd, ws, normed, d_out, act, d_pre, qkv, att,
    ge, gq, gd, gs, tile, bias_e, vec_all, vec_rows,
    wide_e, narrow_e, wide_d, narrow_d, wide_s, narrow_s,
    core_land, ring_land, res_e, res_q, res_d,
    vec_sum, vec_part, vec_came, vec_mine, vec_zy,
    send, recv, core_free, ring_free, wide_free,
):
    low, f32 = jnp.bfloat16, jnp.float32
    z, y, c, x = (lax.axis_index(a) for a in ALL)
    t = c * 4 + x
    copies = Copies(send, recv)
    ws[z, y] = ws_own[...]
    vec_all[z, y, c, x] = vec_own[...]

    own_meta = vec_own[pl.ds(4, 1), :]
    lane = lax.broadcasted_iota(jnp.int32, (1, PAIR), 1)
    own_rank = jnp.sum(jnp.where(lane == 4 + x, own_meta, 0.0), axis=1, keepdims=True)
    own_limit = jnp.sum(jnp.where(lane == 8 + x, own_meta, 0.0), axis=1, keepdims=True)

    def d_out_rows(rows, first):
        row_at = lax.broadcasted_iota(jnp.int32, (16, 1), 0) + first
        live = (row_at.astype(f32) + own_rank * BLOCK < own_limit).astype(f32)
        return cot_ref[rows, :].astype(f32) * live

    def mask_chunk(r, _):
        rows = pl.ds(pl.multiple_of(r * 16, 16), 16)
        d_out[c, x, rows] = d_out_rows(rows, r * 16).astype(low)
        return 0

    lax.fori_loop(0, 8, mask_chunk, 0)
    enter()

    vectors = gather_vectors(copies, vec_all)
    step(vectors)
    shrink = gather_weights(copies, by_rows(ws, 64))
    step(shrink)
    into_expand = expand_to_group(copies, we_send, we, 1024)
    step(into_expand)
    dense_here = copies.start(
        wd_own, wd.at[dense_partner()["z"], dense_partner()["y"]], dense_partner()
    )
    into_qkv = expand_to_group(copies, wq_send, wq, 768)
    step(into_qkv)
    cotangent = gather_tokens(copies, d_out)
    step(cotangent)
    step(vectors)
    step(into_expand)
    expand = gather_weights(copies, by_rows(we, 128))
    step(expand)
    step(shrink)
    step(vectors)
    vec_rows[...] = jnp.zeros_like(vec_rows)
    for d in range(128):
        first = (176 * d) // 128
        vec_rows[pl.ds(first, 3), :] += vec_all[
            d // 32, (d // 8) % 4, (d // 4) % 2, d % 4, pl.ds(0, 3), :
        ]

    def norm_chunk(r, _):
        rows = pl.ds(pl.multiple_of(r * 16, 16), 16)
        values = tokens_ref[rows, :].astype(f32)
        center = values - jnp.mean(values, axis=1, keepdims=True)
        inverse = lax.rsqrt(jnp.mean(center * center, axis=1, keepdims=True) + NORM_EPS)
        own = center * inverse * row_of(vec_rows, 0, 16) + row_of(vec_rows, 16, 16)
        normed[c, x, rows] = own.astype(low)
        return 0

    lax.fori_loop(0, 8, norm_chunk, 0)
    forward = gather_tokens(copies, normed)
    step(forward)
    step(shrink)
    step(expand)
    step(cotangent)
    dense_here.wait_recv()
    dense = gather_weights(copies, by_columns(wd, 2048))
    step(into_qkv)
    qkv_w = gather_weights(copies, by_rows(wq, 128))
    step(expand)
    step(forward)
    step(cotangent)
    step(dense, qkv_w)
    step(shrink)
    step(forward, cotangent)
    step(dense, qkv_w)
    step(expand)
    step(shrink)
    step(dense, qkv_w)
    step(forward)
    step(expand)

    odd = lax.rem(t, 2) == 1
    half = t // 2
    left = lane < HEAD
    bias_e[...] = jnp.zeros_like(bias_e)
    for j in range(8):
        r0 = vec_rows[pl.ds(96 + 8 * j + half, 1), :]
        r1 = vec_rows[pl.ds(100 + 8 * j + half, 1), :]
        even_row = jnp.where(left, r0, pltpu.roll(r1, HEAD, 1))
        odd_row = jnp.where(left, pltpu.roll(r0, HEAD, 1), r1)
        bias_e[pl.ds(0, 1), pl.ds(j * PAIR, PAIR)] = jnp.where(odd, odd_row, even_row)

    def up_tile(i, _):
        g, n = i // 2, lax.rem(i, 2)
        cols = pl.ds(pl.multiple_of(n * 512, 512), 512)
        tile[0] = dot(normed[g].reshape(512, MODEL), we[:, :, :, cols].reshape(MODEL, 512))
        tile[1] = dot_t(d_out[g].reshape(512, MODEL), ws[pl.ds(2 * n, 2)].reshape(512, MODEL))

        def chunk(r, _):
            rows = pl.ds(pl.multiple_of(r * 16, 16), 16)
            pre = tile[0, rows, :] + bias_e[pl.ds(0, 1), cols]
            square = pre * pre
            inner = jnp.tanh(GELU_A * (pre + GELU_B * (square * pre)))
            cover = 0.5 + 0.5 * inner
            act[g, rows, cols] = (pre * cover).astype(low)
            slope = cover + 0.5 * pre * (1.0 - inner * inner) * (
                GELU_A + (3.0 * GELU_A * GELU_B) * square
            )
            d_pre[g, rows, cols] = (tile[1, rows, :] * slope).astype(low)
            return 0

        lax.fori_loop(0, 32, chunk, 0)
        return 0

    lax.fori_loop(0, 2, up_tile, 0)
    step(dense, qkv_w)
    lax.fori_loop(2, 4, up_tile, 0)
    step(dense, qkv_w)

    def shrink_tile(i, _):
        j, n = i // 2, lax.rem(i, 2)
        cols = pl.ds(pl.multiple_of(n * 1024, 1024), 1024)
        mine = act[:, :, pl.ds(pl.multiple_of(j * 512, 512), 512)].reshape(1024, 512)
        term = cross(mine, d_out[:, :, :, cols].reshape(1024, 1024))
        gs[pl.ds(2 * j, 2), :, :, cols] = term.astype(low).reshape(2, 4, 64, 1024)
        return 0

    lax.fori_loop(0, 4, shrink_tile, 0)

    def give_s(part, total):
        gs_out[pl.ds(part * 16, 16), :] = total

    sum_s = scatter_weights(copies, by_rows(gs, 64), wide_s, narrow_s, give_s)
    step(sum_s)

    def grad_tile(left_ref, right_ref, out, width):
        def body(i, _):
            mine = left_ref[:, :, :, pl.ds(pl.multiple_of(i * 512, 512), 512)].reshape(1024, 512)
            term = cross(mine, right_ref[...].reshape(1024, width))
            out[i] = term.astype(low).reshape(4, BLOCK, width)
            return 0

        return body

    expand_tile = grad_tile(normed, d_pre, ge, 1024)
    lax.fori_loop(0, 4, expand_tile, 0)

    def give_e(part, total):
        res_e[pl.ds(2 * part, 2)] = total.astype(low).reshape(2, 16, 1024)

    sum_e = scatter_weights(copies, by_rows(ge, 128), wide_e, narrow_e, give_e)
    step(sum_e)
    step(sum_s)

    def qkv_tile(g, _):
        meta = vec_all[z, y, g, x, pl.ds(4, 1), :]
        projected = dot(normed[g].reshape(512, MODEL), wq[...].reshape(MODEL, 768))
        for p in range(6):
            bias = vec_rows[pl.ds(32 + (p // 2) * 16 + (1 - p % 2) * 8 + t, 1), :]
            for b in range(4):
                rows = pl.ds(b * BLOCK, BLOCK)
                part = projected[b * BLOCK : (b + 1) * BLOCK, p * PAIR : (p + 1) * PAIR] + bias
                if p < 4:
                    part = turned(part, table_of(meta, turn_ref, b), 1)
                part = part.astype(low)
                if p < 2:
                    part = part * jnp.asarray(SCALE, low)
                qkv[g, rows, pl.ds(p * PAIR, PAIR)] = part
        att[g] = dot_t(d_out[g].reshape(512, MODEL), wd[...].reshape(256, MODEL)).astype(low)
        return 0

    lax.fori_loop(0, 2, qkv_tile, 0)
    step(sum_e)
    step(sum_s)

    def attend_tile(i, _):
        g, p = i // 2, lax.rem(i, 2)
        attend(vec_all[z, y, g, x, pl.ds(4, 1), :], turn_ref, qkv, att, g, p)
        return 0

    lax.fori_loop(0, 2, attend_tile, 0)
    step(sum_e)
    step(sum_s)
    lax.fori_loop(2, 4, attend_tile, 0)
    step(sum_s)
    step(sum_e)

    def dense_tile(n, _):
        cols = pl.ds(pl.multiple_of(n * 1024, 1024), 1024)
        term = cross(att[...].reshape(1024, 256), d_out[:, :, :, cols].reshape(1024, 1024))
        gd[:, :, :, cols] = term.astype(low).reshape(4, 4, 16, 1024)
        return 0

    lax.fori_loop(0, 2, dense_tile, 0)

    def give_d(part, total):
        res_d[:, pl.ds(part * 512, 512)] = total.astype(low)

    sum_d = scatter_weights(copies, by_columns(gd, 2048), wide_d, narrow_d, give_d)
    step(sum_d)
    qkv_grad_tile = grad_tile(normed, qkv, gq, 768)
    lax.fori_loop(0, 4, qkv_grad_tile, 0)

    def give_q(part, total):
        res_q[pl.ds(2 * part, 2)] = total.astype(low).reshape(2, 16, 768)

    for _ in sum_e:
        pass
    for axis in ("y", "z"):
        for way in (1, -1):
            to = {axis: other(axis, way)}
            pl.semaphore_signal(wide_free, inc=1, device_id=to, device_id_type=MESH)
    pl.semaphore_wait(wide_free, 4)
    short = pl.ds(0, 768)
    sum_q = scatter_weights(
        copies, by_rows(gq, 128), wide_e.at[:, :, :, :, short], narrow_e.at[:, :, :, short], give_q
    )
    step(sum_q)
    back_e = return_to_group(copies, res_e, ge_out)
    step(back_e)

    for work in (forward, cotangent):
        for _ in work:
            pass

    def down_tile(g):
        def body(i, _):
            cols = pl.ds(pl.multiple_of(i * 512, 512), 512)
            term = dot_t(qkv[g], wq[i].reshape(512, 768)) + dot_t(d_pre[g], we[i].reshape(512, 1024))
            normed[g, :, :, cols] = term.astype(low).reshape(4, BLOCK, 512)
            return 0

        return body

    lax.fori_loop(0, 4, down_tile(1 - c), 0)

    gain = row_of(vec_rows, 0, 16)

    vec_sum[...] = jnp.zeros_like(vec_sum)

    def give_n(rows, total):
        mine = tokens_ref[rows, :].astype(f32)
        middle = mine - jnp.mean(mine, axis=1, keepdims=True)
        spread = lax.rsqrt(jnp.mean(middle * middle, axis=1, keepdims=True) + NORM_EPS)
        xhat = middle * spread
        e = total * gain
        d_in = spread * (
            e - jnp.mean(e, axis=1, keepdims=True) - xhat * jnp.mean(e * xhat, axis=1, keepdims=True)
        )
        dy = d_out_rows(rows, rows.start)
        ig_ref[rows, :] = (dy + d_in).astype(low)
        for i, value in enumerate((total * xhat, total, dy)):
            vec_sum[i] += value[0:8] + value[8:16]

    sum_n = scatter_tokens(copies, normed, core_land, ring_land, give_n, core_free, ring_free, True)
    step(sum_n)
    lax.fori_loop(0, 4, down_tile(c), 0)
    step(sum_d, sum_q)
    step(sum_n)

    def out_tile(g):
        def body(i, _):
            cols = pl.ds(pl.multiple_of(i * 512, 512), 512)
            term = dot(att[g], wd[:, :, :, cols].reshape(256, 512)) + dot(
                act[g], ws[:, :, :, cols].reshape(1024, 512)
            )
            d_out[g, :, :, cols] = term.astype(low).reshape(4, BLOCK, 512)
            return 0

        return body

    lax.fori_loop(0, 4, out_tile(1 - c), 0)
    add_bias = row_of(vec_rows, 80, 16) + row_of(vec_rows, 160, 16)

    def give_o(rows, total):
        out_ref[rows, :] = (tokens_ref[rows, :].astype(f32) + (total + add_bias)).astype(low)

    sum_o = scatter_tokens(copies, d_out, core_land, ring_land, give_o, core_free, ring_free, False)
    step(sum_o)
    step(sum_d, sum_q)
    lax.fori_loop(0, 4, out_tile(c), 0)
    step(sum_n)
    ones = jnp.ones((8, 1024), low)
    vec_mine[...] = jnp.zeros_like(vec_mine)
    vec_mine[pl.ds(3, 1), pl.ds(0, 768)] = dot(ones, qkv[...].reshape(1024, 768))[0:1]
    vec_mine[pl.ds(4, 1), :] = dot(ones, d_pre[...].reshape(1024, 1024))[0:1]
    step(sum_d, sum_q)
    step(sum_n)
    vec_part[...] = jnp.zeros_like(vec_part)
    for i in range(3):
        total = jnp.sum(vec_sum[i], axis=0, keepdims=True)
        for k in range(8):
            vec_part[k, pl.ds(i, 1), :] = total[:, k * 256 : k * 256 + 256]
    sent = []
    for to in token_partners():
        sent.append(copies.start(vec_part.at[to["c"] * 4 + to["x"]], vec_came.at[t], to))
    vec_came[t] = vec_part[t]
    step(sum_o)
    step(sum_d, sum_q)
    back_q = return_to_group(copies, res_q, gq_out)
    step(back_q)
    dense_back = copies.start(res_d, gd_out, dense_partner())
    for copy in sent:
        copy.wait_recv()
    vec_mine[pl.ds(0, 3), pl.ds(0, 256)] = jnp.sum(vec_came[...], axis=0)[0:3]
    vec_zy[z, y] = vec_mine[...]
    sent = [copies.start(vec_mine, vec_zy.at[z, y], to) for to in weight_partners()]
    step(sum_o)
    for copy in sent:
        copy.wait_recv()
    vec_out[c, x] = jnp.sum(vec_zy[...].reshape(16, 8, 1024), axis=0)
    sent = [copies.start(vec_out.at[c, x], vec_out.at[c, x], to) for to in token_partners()]
    step(sum_o)
    step(back_e, back_q)
    dense_back.wait_recv()
    for copy in sent:
        copy.wait_recv()
    for work in (sum_s, sum_e, sum_d, sum_q, sum_n, sum_o, back_e, back_q, vectors, shrink, expand,
                 dense, qkv_w, forward, cotangent, into_expand, into_qkv):
        for _ in work:
            pass
    copies.finish()


def layer(tokens, cotangent, we_send, wq_send, wd_own, ws_own, vec_own):
    low, f32 = jnp.bfloat16, jnp.float32
    vmem = pl.BlockSpec(memory_space=pltpu.VMEM)
    turn = jnp.asarray(np.stack(rotary_constants())[:, : 3 * BLOCK])
    outs = [
        ((BLOCK, MODEL), low), ((BLOCK, MODEL), low), ((8, 16, 1024), low), ((8, 16, 768), low),
        ((16, MODEL), low), ((64, MODEL), f32), ((2, 4, 8, 1024), f32),
    ]
    held = [
        ((4, 4, 128, 1024), low), ((4, 4, 128, 768), low), ((4, 4, 16, 2048), low),
        ((4, 4, 64, 2048), low), ((2, 4, 128, 2048), low), ((2, 4, 128, 2048), low),
        ((2, 512, 1024), low), ((2, 512, 1024), low), ((2, 512, 768), low), ((2, 512, 256), low),
        ((4, 4, 128, 1024), low), ((4, 4, 128, 768), low), ((4, 4, 16, 2048), low),
        ((4, 4, 64, 2048), low), ((2, 512, 512), f32), ((8, 1024), f32),
        ((4, 4, 2, 4, 8, 128), f32), ((184, 128), f32),
        ((2, 6, 4, 32, 1024), low), ((2, 6, 32, 1024), low),
        ((2, 6, 4, 16, 512), low), ((2, 6, 16, 512), low),
        ((2, 6, 4, 16, 2048), low), ((2, 6, 16, 2048), low),
        ((4, 128, 2048), low), ((6, 64, 2048), low),
        ((8, 16, 1024), low), ((8, 16, 768), low), ((16, 2048), low),
        ((3, 8, MODEL), f32), ((8, 8, 256), f32), ((8, 8, 256), f32), ((8, 1024), f32), ((4, 4, 8, 1024), f32),
    ]
    return pl.pallas_call(
        layer_kernel,
        in_specs=[vmem] * 8,
        out_specs=[vmem] * 7,
        out_shape=[jax.ShapeDtypeStruct(s, k) for s, k in outs],
        scratch_shapes=[pltpu.VMEM(s, k) for s, k in held]
        + [
            pltpu.SemaphoreType.DMA((COPIES,)),
            pltpu.SemaphoreType.DMA((COPIES,)),
            pltpu.SemaphoreType.REGULAR,
            pltpu.SemaphoreType.REGULAR,
            pltpu.SemaphoreType.REGULAR,
        ],
        compiler_params=pltpu.CompilerParams(
            collective_id=0, has_side_effects=True, vmem_limit_bytes=64 * 2**20
        ),
        name="layer",
    )(tokens, cotangent, we_send, wq_send, wd_own, ws_own, vec_own, turn)


def adam_step(weight, moment, second, gradient, step_rate, step_decay):
    moment_new = BETA_ONE * moment + (1 - BETA_ONE) * gradient
    second_new = BETA_TWO * second + (1 - BETA_TWO) * gradient * gradient
    moment_hat = moment_new / (1 - BETA_ONE**STEP)
    second_hat = second_new / (1 - BETA_TWO**STEP)
    updated = weight - step_rate * (
        moment_hat / (jnp.sqrt(second_hat) + ADAM_EPS) + step_decay * weight
    )
    return (second_new, updated)


def block_ranks(block_row):
    same = block_row[:, None] == block_row[None, :]
    earlier = jnp.arange(4)[None, :] < jnp.arange(4)[:, None]
    return jnp.sum(jnp.where(same & earlier, 1, 0), axis=1)


def qkv_out(value):
    lead = value.shape[:-1]
    parts = value.reshape(*lead, 3, 2, TPN, PAIR)[..., ::-1, :, :]
    return jnp.moveaxis(parts, -2, 0).reshape(TPN, *lead, 6 * PAIR)


def qkv_back(parts):
    lead = parts.shape[1:-1]
    parts = jnp.moveaxis(parts.reshape(TPN, *lead, 3, 2, PAIR), 0, -2)[..., ::-1, :, :]
    return parts.reshape(*lead, 3 * MODEL)


def expand_out(value):
    lead = value.shape[:-1]
    parts = value.reshape(*lead, FF // 512, TPN, 64)
    return jnp.moveaxis(parts, -2, 0).reshape(TPN, *lead, FF // TPN)


def expand_back(parts):
    lead = parts.shape[1:-1]
    parts = jnp.moveaxis(parts.reshape(TPN, *lead, FF // 512, 64), 0, -2)
    return parts.reshape(*lead, FF)


def to_group(parts):
    return lax.all_to_all(parts, TP, split_axis=0, concat_axis=0, tiled=True)


def placed(value, t):
    return lax.dynamic_update_index_in_dim(
        jnp.zeros((TPN, value.shape[0]), jnp.float32), value, t, axis=0
    )


def dense_route():
    pairs = []
    for z, y, c, x in np.ndindex(*SIZES):
        target = (((1 - z // 2) * 2 + c) * 4 + x) * 8 + (z % 2) * 4 + y
        pairs.append((((z * 4 + y) * 2 + c) * 4 + x, target))
    return pairs


def gathered(value, axes):
    return lax.all_gather(value, axes, axis=0, tiled=True)


def summed(value, axes):
    return lax.psum_scatter(value, axes, scatter_dimension=0, tiled=True)


def shards(
    tokens, cotangent, block_seq, seq_lengths,
    qkv_weight, qkv_moment, qkv_second,
    dense_weight, dense_moment, dense_second,
    expand_weight, expand_moment, expand_second,
    shrink_weight, shrink_moment, shrink_second,
    vectors, vec_moment, vec_second,
):
    z, y, c, x = (lax.axis_index(a) for a in ALL)
    t = c * 4 + x
    low = jnp.bfloat16
    place = ((z * 4 + y) * 8 + t) * 176
    block_row = block_seq[0]
    limits = jnp.where(block_row == 0, seq_lengths[0, 0], seq_lengths[0, 1])
    meta = jnp.concatenate([block_row, block_ranks(block_row), limits]).astype(jnp.float32)
    vec_own = jnp.zeros((1024,), jnp.float32).at[512 : 512 + 12].set(meta)
    vec_own = lax.dynamic_update_slice(
        vec_own, vectors.astype(low).astype(jnp.float32), (lax.rem(place, 128),)
    ).reshape(8, 128)
    output, input_grad, expand_back_rows, qkv_back_rows, dense_rows, shrink_grad, vec_sums = layer(
        tokens,
        cotangent,
        expand_out(expand_weight.astype(low)),
        qkv_out(qkv_weight.astype(low)),
        dense_weight.astype(low),
        shrink_weight.astype(low),
        vec_own,
    )
    expand_grad = expand_back(expand_back_rows).astype(jnp.float32)
    qkv_grad = qkv_back(qkv_back_rows).astype(jnp.float32)
    dense_grad = dense_rows.astype(jnp.float32)
    sums = vec_sums.reshape(TPN, 8, 1024)
    d_out_sum = sums[:, 2, :256].reshape(-1)
    vec_terms = jnp.concatenate(
        [
            sums[:, 0, :256].reshape(-1),
            sums[:, 1, :256].reshape(-1),
            qkv_back(sums[:, 3, :768]),
            d_out_sum,
            expand_back(sums[:, 4]),
            d_out_sum,
        ]
    )
    vec_grad = lax.dynamic_slice(vec_terms, (place,), (176,))

    masters = (qkv_weight, dense_weight, expand_weight, shrink_weight, vectors)
    moments = (qkv_moment, dense_moment, expand_moment, shrink_moment, vec_moment)
    seconds = (qkv_second, dense_second, expand_second, shrink_second, vec_second)
    gradients = (qkv_grad, dense_grad, expand_grad, shrink_grad, vec_grad)
    results = [output, input_grad]
    for i in range(5):
        state_new, weight_new = adam_step(
            masters[i], moments[i], seconds[i], gradients[i], RATES[i], DECAYS[i]
        )
        results.extend([gradients[i], state_new, weight_new])
    return tuple(results)


def solution(mesh):
    finer = Mesh(mesh.devices.reshape(*SIZES), ALL)
    whole, group = P(ALL, None), P(DP, None)
    return jax.shard_map(
        shards,
        mesh=finer,
        in_specs=(whole, whole, group, group, *[whole] * 12, *[P(ALL)] * 3),
        out_specs=(*[whole] * 14, *[P(ALL)] * 3),
        check_vma=False,
    )
```

time: 736 us -> 248 us (0.34)
  waiting for transfers between devices: 465 us -> 0 us
  Pallas kernels: 119 us -> 219 us
  matrix products: 72.5 us -> 0 us
  starting transfers between devices: 18.3 us -> 0 us
  between operations: 15.8 us -> 0.98 us
  other arithmetic: 20.3 us -> 9.49 us
    reduce_scatter x6 -> x0, waiting for transfers between devices: 319 us -> none  [summed(): return lax.psum_scatter(value, axes, scatter_dimension=0, tiled=True)]
    unnamed x8 -> x0, waiting for transfers between devices: 141 us -> none
    pallas_call x2 -> x1, Pallas kernels: 119 us -> 219 us  [layer(): pl.pallas_call(layer_kernel, in_specs=[vmem] * 8, out_specs=[vmem] * 7, o...]
    dot_general x12 -> x0, matrix products: 72.5 us -> none  [the longest x4 26.5 us: cross(): lax.dot_general(a, b, (((0,), (0,)), ((), ())), preferred_element_type=jn...]
    all_to_all x2 -> x0, starting transfers between devices: 13.2 us -> none  [to_group(): return lax.all_to_all(parts, TP, split_axis=0, concat_axis=0, tiled=True)]
  transfers between devices with their start and end apart: 10 -> 0, of which waited for: 8 -> 0; matrix products, arithmetic and copies ran while one was open for 11% -> 0% of each run, Pallas kernels for 0% -> 0%
where the time goes in v3:
time: 248 us
  Pallas kernels  219 us (88%)
  local copies, waits for them, and re-layouts  18.3 us (7%)
  other arithmetic  9.49 us (4%)
    pallas_call x1, Pallas kernels, layer(): pl.pallas_call(layer_kernel, in_specs=[vmem] * 8, out_specs=[vmem] * 7, o...  219 us
    unnamed x69, local copies, waits for them, and re-layouts  9.57 us
    sub x5, other arithmetic, adam_step(): weight - step_rate * (moment_hat / (jnp.sqrt(second_hat) + ADAM_EPS) + st...  5.36 us

profile of v3, /device:TPU:1, one launch (start us, length us, event | category | flops | bytes accessed | tf_op | source)
XLA Modules:
  0.0 247.9 jit_solution(16482817375805838628)
XLA Ops:
  0.7 0.6 copy-done.25
  1.9 0.7 copy-done.26
  2.6 1.3 compare_select_fusion
  4.1 0.7 copy-done.23
  5.5 1.1 convert_element_type.42
  7.2 1.1 reshape.94.we_send
  8.5 1.0 rev.9
  9.5 0.8 reshape.96.wq_send
  10.3 0.7 convert_element_type.45.ws_own
  11.9 219.2 %layer.1 = (bf16[128,2048]{1,0:T(8,128)(2,1)}, bf16[128,2048]{1,0:T(8,128)(2,1)}, bf16[8,16,1024]{2,1,0:T(8,128)(2,1)}, bf16[8,16,768]{2,1,0:T(8,128)(2,1)}, bf1...) custom-call(bf16[128,2048]{1,0:T(8,128)(2,1)} %tokens_ref.1, bf16[128,2048]{1,0:T(8,128)(2,1)} %cot_ref.1, ...), custom_call_target="tpu_custom_call" | custom-call | tf_op jit(solution)/shard_map/layer/pallas_call | solution.py:768
  231.1 1.0 fusion.11
  232.1 1.0 slice.41
  233.1 1.0 slice.43
  234.3 0.6 copy-done.28
  235.0 0.7 multiply_subtract_fusion.4
  237.0 0.6 copy-done.1
  238.0 1.4 multiply_subtract_fusion.1
  239.5 0.8 copy-done.16
  240.6 1.2 multiply_subtract_fusion.2
  242.6 1.4 multiply_subtract_fusion
  243.9 0.8 multiply_subtract_fusion.3
  245.1 0.8 copy.85
  246.3 0.8 copy.86
  247.1 0.8 copy.87
  (81 shorter events, 7.1 us)
Async XLA Ops:
  7.2 1.1 copy-start.5
  8.3 2.0 copy-start.2
  10.3 1.0 copy-start.9
  234.1 1.6 copy-start.17
  234.3 0.7 copy-start.24
  234.3 0.7 copy-start.27
  236.6 1.0 copy-start.1
  236.6 1.2 copy-start.11
  236.6 1.3 copy-start.12
  237.9 1.4 copy-start
  238.0 1.4 copy-start.18
  239.3 1.0 copy-start.16
  239.4 1.1 copy-start.15
  239.5 1.1 copy-start.6
  240.6 1.2 copy-start.3
  240.6 1.4 copy-start.4
  240.6 1.8 copy-start.13
  240.6 1.9 copy-start.14
  242.5 1.4 copy-start.10
  242.6 1.4 copy-start.19
  242.6 1.4 copy-start.20
  242.6 1.4 copy-start.21
  243.9 1.2 copy-start.8
  245.1 1.2 copy-start.7
  (5 other events, 3.3 us)
